TPU v7x, 32 devices: a whole 2x2x4 slice. The times are simulated.
32 devices in a mesh: wide: 16 (over z, x, core), narrow: 2 (over y).
Axes of the slice: x: 2, y: 2, z: 4, core: 2. Of those that a mesh axis runs over, the one named last changes fastest.
Arguments:
- tokens: bfloat16 [1344, 4096], P('wide'), may hold values from -16 to 16
- w_query: bfloat16 [4096, 4096], P('wide', 'narrow'), may hold values from -0.09375 to 0.09375
- w_keyvalue: bfloat16 [4096, 2, 1024], P('wide', None, 'narrow'), may hold values from -0.09375 to 0.09375
- adapter_down: bfloat16 [16, 4096, 2, 512], P('wide', None, None, 'narrow'), may hold values from -0.09375 to 0.09375
- adapter_up_query: bfloat16 [16, 512, 4096], P('wide', None, 'narrow'), may hold values from -0.25 to 0.25
- adapter_up_value: bfloat16 [16, 512, 1024], P('wide', None, 'narrow'), may hold values from -0.25 to 0.25
- request_adapter: int32 [96], P('wide'), may hold values from 0 to 15, as said below
- request_tokens: int32 [96], P('wide'), may hold values from 1 to 14, as said below
- adapter_owner: int32 [16], replicated, may hold values from 0 to 15, each once
Outputs:
- attended: bfloat16 [1344, 4096], P('wide', 'narrow')
Inputs may be any that keep to these rules, and one draw needn't show every extreme that they name: `request_adapter`: the 6 requests of one index of wide name distinct adapters. At most 12 requests name one adapter, and some adapter is named by exactly 12. `request_tokens`: A request's live tokens are the first rows of its slot; each index of wide holds a request with exactly 14. Adapter a's maps are entry adapter_owner[a] of the adapter arrays.
All inputs are finite; a program needn't handle non-finite values.
Results may differ from a plain program's by a relative error of at most 0.012.
Values may be sent and summed in bfloat16 or wider, within the bound.
No kernel may reach another device: no remote copies, remote signals or barrier semaphores. Data moves between devices by JAX's collectives and lax.ppermute only.
A program may use at most 128 MiB of HBM per device.

v0:
```python
import math

import jax
import jax.numpy as jnp
from jax import lax
from jax.sharding import PartitionSpec as P

HD = 128
REQ_LEN = 14


rope_theta = 500000.0


def rope_tables(length, head_size):
    half_size = head_size // 2
    exponent = jnp.arange(half_size, dtype=jnp.float32) * (2.0 / head_size)
    frequency = rope_theta ** (-exponent)
    angles = jnp.arange(length, dtype=jnp.float32)[:, None] * frequency[None, :]
    angles = jnp.concatenate([angles, angles], axis=1)
    return (jnp.cos(angles), jnp.sin(angles))


def rotate(values, cosine, sine_table):
    half_size = values.shape[-1] // 2
    turned = jnp.concatenate([-values[..., half_size:], values[..., :half_size]], axis=-1)
    return values * cosine[:, None, :] + turned * sine_table[:, None, :]


def attend(queries, key_rows, value_rows, counts):
    length = queries.shape[1]
    scores = jnp.einsum("rikgd,rjkd->rkgij", queries, key_rows, preferred_element_type=jnp.float32)
    scores = scores * (1.0 / math.sqrt(queries.shape[-1]))
    position = jnp.arange(length, dtype=jnp.int32)
    causal = position[None, :] <= position[:, None]
    allowed = causal[None, :, :] & (position[None, None, :] < counts[:, None, None])
    scores = jnp.where(allowed[:, None, None, :, :], scores, -1e30)
    row_max = jnp.max(scores, axis=-1, keepdims=True)
    numerators = jnp.exp(scores - row_max)
    probabilities = (numerators / jnp.sum(numerators, axis=-1, keepdims=True)).astype(jnp.bfloat16)
    mixture = jnp.einsum(
        "rkgij,rjkd->rikgd", probabilities, value_rows, preferred_element_type=jnp.float32
    )
    live_rows = position[None, :] < counts[:, None]
    mixture = jnp.where(live_rows[:, :, None, None, None], mixture, 0.0)
    return mixture.astype(jnp.bfloat16)


def body(
    tokens,
    w_query,
    w_keyvalue,
    adapter_down,
    adapter_up_query,
    adapter_up_value,
    request_adapter,
    request_tokens,
    adapter_owner,
):
    wide_count = lax.axis_size("wide")
    narrow_count = lax.axis_size("narrow")
    narrow_index = lax.axis_index("narrow")
    tok_rows = tokens.shape[0]
    width_model = tokens.shape[1]
    requests_here = tok_rows // REQ_LEN
    capacity = 2 * requests_here
    slice_width = width_model // narrow_count
    query_cols = w_query.shape[1]
    key_cols = w_keyvalue.shape[2]
    local_rank = adapter_down.shape[3]
    row_total = capacity * REQ_LEN
    table_index = jnp.arange(adapter_owner.shape[0], dtype=jnp.int32)
    matches = request_adapter[:, None] == table_index[None, :]
    my_groups = jnp.sum(jnp.where(matches, adapter_owner[None, :], 0), axis=1)
    dest_select = (my_groups[None, :] == jnp.arange(wide_count, dtype=jnp.int32)[:, None]).astype(
        jnp.bfloat16
    )
    own_slice = lax.dynamic_slice_in_dim(tokens, narrow_index * slice_width, slice_width, 1)
    own_slice = own_slice.reshape(requests_here, REQ_LEN, slice_width)
    outgoing = jnp.einsum(
        "dr,rlf->dlf", dest_select, own_slice, preferred_element_type=jnp.float32
    ).astype(jnp.bfloat16)
    out_flags = jnp.sum(dest_select.astype(jnp.float32), axis=1, keepdims=True).astype(jnp.bfloat16)
    arrived, arrived_flags = (
        lax.all_to_all(outgoing, "wide", split_axis=0, concat_axis=0, tiled=True),
        lax.all_to_all(out_flags, "wide", split_axis=0, concat_axis=0, tiled=True),
    )
    query_piece = lax.all_gather(w_query, "wide", axis=0, tiled=True)
    keyvalue_piece = lax.all_gather(w_keyvalue, "wide", axis=0, tiled=True)
    query_sum = jnp.dot(tokens, query_piece, preferred_element_type=jnp.float32)
    flat_piece = keyvalue_piece.reshape(keyvalue_piece.shape[0], 2 * key_cols)
    keyvalue_sum = jnp.dot(tokens, flat_piece, preferred_element_type=jnp.float32)
    query_base = query_sum
    incoming = (arrived_flags[:, 0] > 0.5).astype(jnp.int32)
    arrival_rank = jnp.cumsum(incoming) - 1
    slot_index = jnp.arange(capacity, dtype=jnp.int32)[:, None]
    compact_select = ((incoming[None, :] == 1) & (arrival_rank[None, :] == slot_index)).astype(
        jnp.bfloat16
    )
    compacted = jnp.einsum(
        "kh,hlf->klf", compact_select, arrived, preferred_element_type=jnp.float32
    ).astype(jnp.bfloat16)
    held_rows = compacted.reshape(row_total, slice_width)
    down_local = adapter_down[0].reshape(width_model, 2 * local_rank)
    shrunk = jnp.dot(
        lax.all_gather(held_rows, "narrow", axis=1, tiled=True),
        down_local,
        preferred_element_type=jnp.float32,
    )
    shrunk = shrunk.reshape(row_total, 2, local_rank)
    shrunk = shrunk.astype(jnp.bfloat16)
    up_query = adapter_up_query[0]
    up_value = adapter_up_value[0]
    rank_piece = lax.all_gather(shrunk, "narrow", axis=2, tiled=True)
    query_sum = jnp.dot(rank_piece[:, 0, :], up_query, preferred_element_type=jnp.float32)
    value_sum = jnp.dot(rank_piece[:, 1, :], up_value, preferred_element_type=jnp.float32)
    deltas = jnp.concatenate([query_sum, value_sum], axis=1).astype(jnp.bfloat16)
    deltas = deltas.reshape(capacity, REQ_LEN, query_cols + key_cols)
    going_back = jnp.einsum(
        "kh,klc->hlc", compact_select, deltas, preferred_element_type=jnp.float32
    ).astype(jnp.bfloat16)
    returned = lax.all_to_all(going_back, "wide", split_axis=0, concat_axis=0, tiled=True)
    own_deltas = jnp.einsum(
        "dr,dlc->rlc", dest_select, returned, preferred_element_type=jnp.float32
    )
    cosine, sine_table = rope_tables(REQ_LEN, HD)
    local_heads = query_cols // HD
    local_kv = key_cols // HD
    queries = query_base.reshape(requests_here, REQ_LEN, query_cols) + own_deltas[:, :, :query_cols]
    queries = rotate(
        queries.reshape(requests_here, REQ_LEN, local_heads, HD), cosine, sine_table
    ).astype(jnp.bfloat16)
    key_rows = rotate(
        keyvalue_sum[:, :key_cols].reshape(requests_here, REQ_LEN, local_kv, HD), cosine, sine_table
    ).astype(jnp.bfloat16)
    value_rows = (
        keyvalue_sum[:, key_cols:].reshape(requests_here, REQ_LEN, key_cols)
        + own_deltas[:, :, query_cols:]
    )
    value_rows = value_rows.reshape(requests_here, REQ_LEN, local_kv, HD).astype(jnp.bfloat16)
    grouped = queries.reshape(requests_here, REQ_LEN, local_kv, local_heads // local_kv, HD)
    result = attend(grouped, key_rows, value_rows, request_tokens)
    return result.reshape(tok_rows, query_cols)


def solution(mesh):
    return jax.shard_map(
        body,
        mesh=mesh,
        in_specs=(
            P("wide", None),
            P("wide", "narrow"),
            P("wide", None, "narrow"),
            P("wide", None, None, "narrow"),
            P("wide", None, "narrow"),
            P("wide", None, "narrow"),
            P("wide"),
            P("wide"),
            P(),
        ),
        out_specs=P("wide", "narrow"),
        check_vma=False,
    )
```

profile of v0, /device:TPU:0, one launch (start us, length us, event | category | flops | bytes accessed | tf_op | source)
XLA Modules:
  0.0 324.5 jit_solution(11448428825684928947)
XLA Ops:
  6.5 1.0 select_reduce_fusion
  7.5 0.1 fusion.48
  7.6 0.7 copy.104
  8.3 7.4 %all-to-all-start = ((bf16[16,1,1]{2,1,0:T(2,128)(2,1)}), bf16[16,1,1]{2,1,0:T(2,128)(2,1)S(1)}, u32[]{:S(2)}, u32[]{:S(2)}) async-start(bf16[16,1,1]{2,1,0:T(2,128)(2,1)} %copy.104), calls=%async_computation | async-start | bytes 16384 | tf_op jit(solution)/shard_map/all_to_all | solution.py:86
  15.7 1.0 constant_dynamic-slice_fusion
  16.7 0.1 reshape.213
  16.8 0.6 convolution_convert_fusion.1
  17.4 1.5 copy.107
  18.9 3.1 all-to-all-done
  22.0 3.7 %all-to-all-start.1 = ((bf16[16,14,2048]{2,1,0:T(8,128)(2,1)}), bf16[16,14,2048]{2,1,0:T(8,128)(2,1)S(1)}, u32[]{:S(2)}, u32[]{:S(2)}) async-start(bf16[16,14,2048]{2,1,0:T(8,128)(2,1)} %copy.107), calls=%async_computation.1 | async-start | bytes 2097152 | tf_op jit(solution)/shard_map/all_to_all | solution.py:85
  25.7 0.0 all-gather.6.cloned.1.call-start
  25.7 0.4 compare_reduce_fusion
  26.2 0.1 add_reduce_fusion
  26.3 22.3 %all-to-all-done.1 = bf16[16,14,2048]{2,1,0:T(8,128)(2,1)S(1)} async-done(((bf16[16,14,2048]{2,1,0:T(8,128)(2,1)}), bf16[16,14,2048]{2,1,0:T(8,128)(2,1)S(1)}, u32[]{:S(2)}, u32[]{:S(2)}) %all-to-all-start.1) | async-done | bytes 917536 | tf_op jit(solution)/shard_map/all_to_all | solution.py:85
  48.6 1.2 convolution_convert_fusion.2
  49.8 0.4 copy.110
  50.2 1.1 reshape.214
  51.2 0.0 all-gather.6.cloned.1.call-update
  51.3 0.0 all-gather.4.cloned.1.call-start
  51.3 0.7 all-gather.4.cloned.1.call-update
  52.0 0.0 all-gather.8.cloned.1.call-start
  52.1 0.7 all-gather.8.cloned.1.call-update
  52.8 4.8 %copy.134 = bf16[512,8,2,256]{3,1,2,0:T(8,128)(2,1)} copy(bf16[512,8,2,256]{3,2,1,0:T(2,128)(2,1)} %bitcast.69) | data formatting | bytes 8388608
  57.6 6.5 %copy.111 = bf16[512,4096]{1,0:T(8,128)(2,1)} copy(bf16[512,4096]{0,1:T(8,128)(2,1)} %bitcast.67) | data formatting | bytes 8388608 | tf_op jit(solution)/shard_map/dot_general | solution.py:105
  64.1 14.5 %all-gather.6.cloned.1.call-done = bf16[168,4096]{1,0:T(8,128)(2,1)} async-done(((bf16[168,2048]{1,0:T(8,128)(2,1)}), bf16[168,4096]{1,0:T(8,128)(2,1)}) %all-gather.6.cloned.1.call-update) | async-done | bytes 1376272 | tf_op jit(solution)/shard_map/all_gather | solution.py:106
  78.6 4.2 %fusion.10 = bf16[168,2,256]{2,0,1:T(8,128)(2,1)S(1)} fusion(bf16[2,256,4096]{2,1,0:T(8,128)(2,1)} %bitcast.70, bf16[168,4096]{1,0:T(8,128)(2,1)} %all-gather.6.cloned.1.call-done), kind=kOutput, calls=%fused_computation.17 | convolution fusion | flops 704729088 | bytes 5742592 | tf_op jit(solution)/shard_map/dot_general | solution.py:105
  82.7 0.0 copy-start.4
  82.7 6.9 %all_gather.14 = bf16[168,2,512]{2,0,1:T(8,128)(2,1)S(1)} all-gather(bf16[168,2,256]{2,0,1:T(8,128)(2,1)S(1)} %fusion.10), channel_id=1, replica_groups=mesh['wide'=16,'narrow'=2] {'narrow'}, dimensions={2}, use_global_device_ids=true | all-gather | bytes 516096 | tf_op jit(solution)/shard_map/all_gather | solution.py:114
  89.7 0.1 dot_general.47
  89.8 0.1 dot_general.49
  89.8 0.3 convolution_convert_fusion.4
  90.1 0.6 convolution_convert_fusion.3
  90.7 0.1 pad_maximum_fusion
  90.8 1.1 convolution_convert_fusion
  91.9 0.0 copy-start.5
  91.9 1.8 copy.113
  93.7 5.8 %all-to-all-start.2 = ((bf16[16,14,2560]{2,1,0:T(8,128)(2,1)}), bf16[16,14,2560]{2,1,0:T(8,128)(2,1)S(1)}, u32[]{:S(2)}, u32[]{:S(2)}) async-start(bf16[16,14,2560]{2,1,0:T(8,128)(2,1)} %copy.113), calls=%async_computation.2 | async-start | bytes 2621440 | tf_op jit(solution)/shard_map/all_to_all | solution.py:122
  99.5 0.1 fusion.37
  99.6 0.1 iota_compare_fusion.4
  99.7 0.1 broadcast_and_fusion
  99.8 42.6 %all-to-all-done.2 = bf16[16,14,2560]{2,1,0:T(8,128)(2,1)S(1)} async-done(((bf16[16,14,2560]{2,1,0:T(8,128)(2,1)}), bf16[16,14,2560]{2,1,0:T(8,128)(2,1)S(1)}, u32[]{:S(2)}, u32[]{:S(2)}) %all-to-all-start.2) | async-done | bytes 1146912 | tf_op jit(solution)/shard_map/all_to_all | solution.py:122
  142.4 1.3 fusion.13
  143.8 29.8 %all-gather.4.cloned.1.call-done = bf16[4096,2,512]{2,1,0:T(2,128)(2,1)} async-done(((bf16[256,2,512]{2,1,0:T(2,128)(2,1)}), bf16[4096,2,512]{2,1,0:T(2,128)(2,1)}) %all-gather.4.cloned.1.call-update) | async-done | bytes 8388624 | tf_op jit(solution)/shard_map/all_gather | solution.py:89
  173.6 9.7 %copy.133 = bf16[512,8,2,512]{3,1,2,0:T(8,128)(2,1)} copy(bf16[512,8,2,512]{3,2,1,0:T(2,128)(2,1)} %bitcast.68) | data formatting | bytes 16777216
  183.2 5.2 %fusion.67 = f32[84,1024]{1,0:T(8,128)S(1)} fusion(bf16[84,4096]{1,0:T(8,128)(2,1)S(1)} %copy-done.2, bf16[4096,1024]{1,0:T(8,128)(2,1)} %bitcast.66), kind=kOutput, calls=%fused_computation.79 | convolution fusion | flops 704643072 | bytes 9420800 | tf_op jit(solution)/shard_map/dot_general | solution.py:92
  188.5 0.1 reshape.215
  188.6 0.8 slice-done
  189.4 0.1 fusion.24
  189.5 0.1 slice_negate_fusion.1
  189.7 111.8 %all-gather.8.cloned.1.call-done = bf16[4096,2048]{1,0:T(8,128)(2,1)} async-done(((bf16[256,2048]{1,0:T(8,128)(2,1)}), bf16[4096,2048]{1,0:T(8,128)(2,1)}) %all-gather.8.cloned.1.call-update) | async-done | bytes 16777232 | tf_op jit(solution)/shard_map/all_gather | solution.py:88
  301.5 9.4 %fusion.68 = f32[84,2048]{1,0:T(8,128)} fusion(bf16[84,4096]{1,0:T(8,128)(2,1)S(1)} %copy-done.2, bf16[4096,2048]{1,0:T(8,128)(2,1)} %all-gather.8.cloned.1.call-done), kind=kOutput, calls=%fused_computation.80 | convolution fusion | flops 1409286144 | bytes 18153472 | tf_op jit(solution)/shard_map/dot_general | solution.py:90
  311.0 1.3 reshape.216
  312.2 0.1 slice-done.1
  312.3 0.4 copy_add_fusion
  312.8 0.1 reshape.218
  312.9 0.5 reshape.217
  313.4 0.3 slice_negate_fusion
  313.7 0.5 fusion.18
  314.2 1.1 fusion.62
  315.3 1.1 fusion.7
  316.4 0.5 fusion.9
  316.9 0.1 copy.123
  317.0 0.9 reshape.219
  317.9 0.0 copy-done.1
  (20 shorter events, 0.2 us)
Async XLA Ops:
  6.5 83.6 %copy-start = (bf16[1,512,2048]{2,1,0:T(8,128)(2,1)S(1)}, bf16[1,512,2048]{2,1,0:T(8,128)(2,1)}, u32[]{:S(2)}) copy-start(bf16[1,512,2048]{2,1,0:T(8,128)(2,1)} %param.13) | copy-start | bytes 6291460
  8.3 13.7 %all-to-all-start = ((bf16[16,1,1]{2,1,0:T(2,128)(2,1)}), bf16[16,1,1]{2,1,0:T(2,128)(2,1)S(1)}, u32[]{:S(2)}, u32[]{:S(2)}) async-start(bf16[16,1,1]{2,1,0:T(2,128)(2,1)} %copy.104), calls=%async_computation | async-start | bytes 16384 | tf_op jit(solution)/shard_map/all_to_all | solution.py:86
  22.0 26.6 %all-to-all-start.1 = ((bf16[16,14,2048]{2,1,0:T(8,128)(2,1)}), bf16[16,14,2048]{2,1,0:T(8,128)(2,1)S(1)}, u32[]{:S(2)}, u32[]{:S(2)}) async-start(bf16[16,14,2048]{2,1,0:T(8,128)(2,1)} %copy.107), calls=%async_computation.1 | async-start | bytes 2097152 | tf_op jit(solution)/shard_map/all_to_all | solution.py:85
  25.7 52.9 %all-gather.6.cloned.1.call-start = ((), (), s32[]{:S(2)}) async-start(), calls=%async_computation.4 | async-start | bytes 2064384 | tf_op jit(solution)/shard_map/all_gather | solution.py:106
  51.3 122.3 %all-gather.4.cloned.1.call-start = ((), (), s32[]{:S(2)}) async-start(), calls=%async_computation.3 | async-start | bytes 8912896 | tf_op jit(solution)/shard_map/all_gather | solution.py:89
  52.0 249.5 %all-gather.8.cloned.1.call-start = ((), (), s32[]{:S(2)}) async-start(), calls=%async_computation.5 | async-start | bytes 17825792 | tf_op jit(solution)/shard_map/all_gather | solution.py:88
  82.7 7.1 %copy-start.4 = (bf16[1,512,512]{2,1,0:T(8,128)(2,1)S(1)}, bf16[1,512,512]{2,1,0:T(8,128)(2,1)}, u32[]{:S(2)}) copy-start(bf16[1,512,512]{2,1,0:T(8,128)(2,1)} %param.14) | copy-start | bytes 1572868
  91.9 7.8 %copy-start.5 = (s32[6]{0:T(128)S(1)}, s32[6]{0:T(128)}, u32[]{:S(2)}) copy-start(s32[6]{0:T(128)} %param.16) | copy-start | bytes 76
  93.7 48.8 %all-to-all-start.2 = ((bf16[16,14,2560]{2,1,0:T(8,128)(2,1)}), bf16[16,14,2560]{2,1,0:T(8,128)(2,1)S(1)}, u32[]{:S(2)}, u32[]{:S(2)}) async-start(bf16[16,14,2560]{2,1,0:T(8,128)(2,1)} %copy.113), calls=%async_computation.2 | async-start | bytes 2621440 | tf_op jit(solution)/shard_map/all_to_all | solution.py:122
  143.8 39.5 %copy-start.3 = (f32[6,14,2560]{2,0,1:T(8,128)}, f32[6,14,2560]{2,0,1:T(8,128)S(1)}, u32[]{:S(2)}) copy-start(f32[6,14,2560]{2,0,1:T(8,128)S(1)} %fusion.13) | copy-start | bytes 2580484
  173.6 9.7 %copy-start.2 = (bf16[84,4096]{1,0:T(8,128)(2,1)S(1)}, bf16[84,4096]{1,0:T(8,128)(2,1)}, u32[]{:S(2)}) copy-start(bf16[84,4096]{1,0:T(8,128)(2,1)} %param.9) | copy-start | bytes 2064388
  188.4 0.9 slice-start
  310.9 1.4 slice-start.1
  316.4 1.6 copy-start.1
Sparse Core Ops, SparseCore 0:
  51.4 27.1 all-gather.5
  80.7 92.7 all-gather.3
  175.7 125.7 all-gather.7
where the time goes:
time: 325 us
  waiting for transfers between devices  226 us (70%)
  local copies, waits for them, and re-layouts  31.8 us (10%)
  matrix products  26.5 us (8%)
  starting transfers between devices  16.9 us (5%)
  between operations  13.4 us (4%)
  blocking collectives  6.93 us (2%)
  other arithmetic  3.44 us (1%)
    all_gather x1, waiting for transfers between devices, body(): query_piece = lax.all_gather(w_query, 'wide', axis=0, tiled=True)  112 us
    all_to_all x1, waiting for transfers between devices, body(): lax.all_to_all(going_back, 'wide', split_axis=0, concat_axis=0, tiled=True)  42.6 us
    all_gather x1, waiting for transfers between devices, body(): keyvalue_piece = lax.all_gather(w_keyvalue, 'wide', axis=0, tiled=True)  29.8 us
    all_to_all x1, waiting for transfers between devices, body(): lax.all_to_all(outgoing, 'wide', split_axis=0, concat_axis=0, tiled=True)  22.3 us
    unnamed x14, local copies, waits for them, and re-layouts  14.6 us
    all_gather x1, waiting for transfers between devices, body(): lax.all_gather(held_rows, 'narrow', axis=1, tiled=True)  14.5 us
    dot_general x1, matrix products, body(): query_sum = jnp.dot(tokens, query_piece, preferred_element_type=jnp.float32)  9.44 us
    all_to_all x1, starting transfers between devices, body(): lax.all_to_all(out_flags, 'wide', split_axis=0, concat_axis=0, tiled=True)  7.36 us
  transfers between devices with their start and end apart: 6, of which 6 were waited for; matrix products, arithmetic and copies ran while one was open for 12% of the time, Pallas kernels for 0%

commit v1 on v0

--- a/solution.py
+++ b/solution.py
@@ -1,15 +1,23 @@
+import functools
 import math
 
 import jax
 import jax.numpy as jnp
+import numpy as np
 from jax import lax
+from jax.experimental import pallas as pl
+from jax.experimental.pallas import tpu as pltpu
+from jax.sharding import Mesh
 from jax.sharding import PartitionSpec as P
 
 HD = 128
 REQ_LEN = 14
-
+SLOT = 16
+PLANE = 4
 
 rope_theta = 500000.0
+BF16 = jnp.bfloat16
+F32 = jnp.float32
 
 
 def rope_tables(length, head_size):
@@ -46,7 +54,7 @@
     return mixture.astype(jnp.bfloat16)
 
 
-def body(
+def gather_body(
     tokens,
     w_query,
     w_keyvalue,
@@ -87,10 +95,9 @@
     )
     query_piece = lax.all_gather(w_query, "wide", axis=0, tiled=True)
     keyvalue_piece = lax.all_gather(w_keyvalue, "wide", axis=0, tiled=True)
-    query_sum = jnp.dot(tokens, query_piece, preferred_element_type=jnp.float32)
+    query_base = jnp.dot(tokens, query_piece, preferred_element_type=jnp.float32)
     flat_piece = keyvalue_piece.reshape(keyvalue_piece.shape[0], 2 * key_cols)
     keyvalue_sum = jnp.dot(tokens, flat_piece, preferred_element_type=jnp.float32)
-    query_base = query_sum
     incoming = (arrived_flags[:, 0] > 0.5).astype(jnp.int32)
     arrival_rank = jnp.cumsum(incoming) - 1
     slot_index = jnp.arange(capacity, dtype=jnp.int32)[:, None]
@@ -107,13 +114,14 @@
         down_local,
         preferred_element_type=jnp.float32,
     )
-    shrunk = shrunk.reshape(row_total, 2, local_rank)
-    shrunk = shrunk.astype(jnp.bfloat16)
-    up_query = adapter_up_query[0]
-    up_value = adapter_up_value[0]
+    shrunk = shrunk.reshape(row_total, 2, local_rank).astype(jnp.bfloat16)
     rank_piece = lax.all_gather(shrunk, "narrow", axis=2, tiled=True)
-    query_sum = jnp.dot(rank_piece[:, 0, :], up_query, preferred_element_type=jnp.float32)
-    value_sum = jnp.dot(rank_piece[:, 1, :], up_value, preferred_element_type=jnp.float32)
+    query_sum = jnp.dot(
+        rank_piece[:, 0, :], adapter_up_query[0], preferred_element_type=jnp.float32
+    )
+    value_sum = jnp.dot(
+        rank_piece[:, 1, :], adapter_up_value[0], preferred_element_type=jnp.float32
+    )
     deltas = jnp.concatenate([query_sum, value_sum], axis=1).astype(jnp.bfloat16)
     deltas = deltas.reshape(capacity, REQ_LEN, query_cols + key_cols)
     going_back = jnp.einsum(
@@ -143,21 +151,536 @@
     return result.reshape(tok_rows, query_cols)
 
 
+VMEM = pl.BlockSpec(memory_space=pltpu.VMEM)
+SMEM = pl.BlockSpec(memory_space=pltpu.SMEM)
+PARAMS = pltpu.CompilerParams(vmem_limit_bytes=16 * 2**20)
+
+ORDER = ((3, 2, 1, 0), (3, 2, 0, 1), (0, 1, 3, 2), (0, 1, 2, 3))
+SEND2 = (1, 0, 0, 1)
+INWARD, MIDDLE, PAIRS = ((0, 1), (3, 2)), ((1, 2), (2, 1)), ((0, 1), (1, 0), (2, 3), (3, 2))
+
+
+def call(kernel, out_shape, ins, flops=0, nbytes=0, scratch=(), name=None):
+    arrays = [a for a, _ in ins]
+    specs = [s for _, s in ins]
+    many = isinstance(out_shape, (list, tuple))
+    return pl.pallas_call(
+        kernel,
+        out_shape=out_shape,
+        in_specs=specs,
+        out_specs=[VMEM] * len(out_shape) if many else VMEM,
+        scratch_shapes=list(scratch),
+        compiler_params=PARAMS,
+        cost_estimate=pl.CostEstimate(flops=flops, bytes_accessed=nbytes, transcendentals=0),
+        name=name,
+    )(*arrays)
+
+
+def iota(shape, axis):
+    return lax.broadcasted_iota(jnp.int32, shape, axis)
+
+
+def over_len(index):
+    return (index * 4682) >> 16
+
+
+def dot(a, b, contract=((1,), (0,))):
+    return lax.dot_general(a, b, (contract, ((), ())), preferred_element_type=F32)
+
+
+def dispatch_kernel(requests_here, pos, tokens, slots, filled, sems):
+    count, _, half = filled.shape
+    columns = pl.ds(pl.multiple_of(pos[2] * half, half), half)
+    filled[...] = jnp.zeros(filled.shape, filled.dtype)
+    for r in range(requests_here):
+        owner = pos[3 + requests_here + pos[3 + r]]
+        filled[owner, 0:REQ_LEN, :] = tokens[r * REQ_LEN : (r + 1) * REQ_LEN, columns]
+        mark = (iota((SLOT - REQ_LEN, 128), 0) == 0) & (iota((SLOT - REQ_LEN, 128), 1) == r)
+        filled[owner, REQ_LEN:SLOT, 0:128] = mark.astype(F32).astype(BF16)
+    copies = [
+        pltpu.make_async_copy(filled.at[n], slots.at[n], sems.at[n]) for n in range(count)
+    ]
+    for copy in copies:
+        copy.start()
+    for copy in copies:
+        copy.wait()
+
+
+def slices_kernel(pos, tokens, *slices):
+    z, q = pos[0], pos[1]
+    count = len(slices)
+    depth = slices[0].shape[1] // PLANE
+    for shift, out in enumerate(slices):
+        to = (z + shift) & (count - 1)
+        for i in range(PLANE):
+            start = pl.multiple_of((to * PLANE + (q ^ i)) * depth, depth)
+            out[:, i * depth : (i + 1) * depth] = tokens[:, pl.ds(start, depth)]
+
+
+def compact_kernel(pos, order, arrived, packed, select, marks):
+    z, q = pos[0], pos[1]
+    count = arrived.shape[0]
+    rows = count * SLOT
+    blocks = []
+    for o in range(count):
+        home = order[z, o // PLANE] * PLANE + (q ^ (o % PLANE))
+        blocks.append(arrived[home])
+    held = jnp.concatenate(blocks, axis=0)
+    here = (iota((rows, 128), 0) & (SLOT - 1)) == REQ_LEN
+    marked = jnp.where(here, held[:, :128].astype(F32), 0.0)
+    marked = jnp.where(iota((rows, 128), 1) < 8, marked, 0.0).astype(BF16)
+    marks[...] = marked
+    row, col = iota((rows, rows), 0), iota((rows, rows), 1)
+    same = ((row >> 4) == (col >> 4)).astype(F32).astype(BF16)
+    which = dot(marked, same, ((0,), (0,)))
+    present = jnp.sum(which, axis=0, keepdims=True)
+    earlier = (((row & (SLOT - 1)) == 0) & ((row >> 4) < (col >> 4))).astype(F32).astype(BF16)
+    rank = dot(jnp.broadcast_to(present, (8, rows)).astype(BF16), earlier)[:1]
+    out_rows = packed.shape[0]
+    k = over_len(iota((out_rows, rows), 0))
+    place = iota((out_rows, rows), 0) - k * REQ_LEN
+    chosen = (k.astype(F32) == rank) & (present > 0.5)
+    chosen = chosen & (place == (iota((out_rows, rows), 1) & (SLOT - 1)))
+    chosen = chosen.astype(F32).astype(BF16)
+    select[...] = chosen
+    packed[...] = dot(chosen, held).astype(BF16)
+
+
+def shrink_kernel(pos, own, down, total):
+    half = own.shape[1]
+    mine = pl.ds(pl.multiple_of(pos[2] * half, half), half)
+    total[...] = dot(own[...], down[mine, :])
+
+
+def shrink_rest_kernel(pos, total, other, down, out):
+    half = other.shape[1]
+    theirs = pl.ds(pl.multiple_of((1 - pos[2]) * half, half), half)
+    rows = total.shape[0]
+    out[rows:, :] = jnp.zeros((out.shape[0] - rows, out.shape[1]), BF16)
+    out[0:rows, :] = (total[...] + dot(other[...], down[theirs, :])).astype(BF16)
+
+
+def expand_kernel(pos, own, other, select, marks, up_query, up_value, *outs):
+    y = pos[2]
+    rank = own.shape[1] // 2
+    mine = pl.ds(pl.multiple_of(y * rank, rank), rank)
+    theirs = pl.ds(pl.multiple_of((1 - y) * rank, rank), rank)
+    chosen = select[...]
+    rows = chosen.shape[0]
+    own_rows = dot(chosen, own[0:rows, :], ((0,), (0,))).astype(BF16)
+    other_rows = dot(chosen, other[0:rows, :], ((0,), (0,))).astype(BF16)
+    query_cols = up_query.shape[1]
+    for name, up, first in ((0, up_query, 0), (1, up_value, query_cols)):
+        span = slice(name * rank, (name + 1) * rank)
+        delta = dot(own_rows[:, span], up[mine, :]) + dot(other_rows[:, span], up[theirs, :])
+        if name == 0:
+            head = delta[:, :128] + marks[...].astype(F32)
+            delta = jnp.concatenate([head, delta[:, 128:]], axis=1)
+        delta = delta.astype(BF16)
+        for i in range(PLANE):
+            for b in range(4):
+                start = (b * PLANE + i) * SLOT
+                piece = delta[start : start + SLOT]
+                out = outs[min(b, 2) * PLANE + i]
+                at = max(b - 2, 0) * SLOT
+                out[at : at + SLOT, first : first + up.shape[1]] = piece
+
+
+def partial_kernel(pos, inverse, s0, s1, s2, s3, q0, q1, q2, q3, v0, v1, v2, v3, out_a, out_b, rows):
+    z = pos[0]
+    count, height, _ = out_a.shape
+    padded = rows.shape[0] // count
+    rows[...] = jnp.zeros(rows.shape, rows.dtype)
+    for shift, s in enumerate((s0, s1, s2, s3)):
+        rows[shift * padded : shift * padded + height, :] = s[...]
+    tile = 512
+    queries, values = (q0, q1, q2, q3), (v0, v1, v2, v3)
+    spans = [(queries, n * tile) for n in range(q0.shape[1] // tile)]
+    half = v0.shape[1] // 2
+    spans += [(values, half + n * tile) for n in range(half // tile)]
+    spans += [(values, n * tile) for n in range(half // tile)]
+    for n, (refs, start) in enumerate(spans):
+        weights = jnp.concatenate([r[:, start : start + tile] for r in refs], axis=0)
+        total = dot(rows[...], weights)
+        at = n * tile
+        out, at = (out_a, at) if at < out_a.shape[2] else (out_b, at - out_a.shape[2])
+        for shift in range(count):
+            block = total[shift * padded : shift * padded + height]
+            out[inverse[z, shift], :, at : at + tile] = block
+
+
+def placed(height, pieces):
+    held = jnp.concatenate(pieces, axis=0)
+    rows = held.shape[0]
+    here = (iota((rows, 128), 0) & (SLOT - 1)) == REQ_LEN
+    marked = jnp.where(here, held[:, :128].astype(F32), 0.0).astype(BF16)
+    same = ((iota((rows, rows), 0) >> 4) == (iota((rows, rows), 1) >> 4)).astype(F32).astype(BF16)
+    which = dot(marked, same, ((0,), (0,))).astype(BF16)
+    request = over_len(iota((height, 128), 0))
+    chosen = dot((request == iota((height, 128), 1)).astype(F32).astype(BF16), which)
+    t = iota((height, rows), 0)
+    place = t - over_len(t) * REQ_LEN
+    chosen = jnp.where(place == (iota((height, rows), 1) & (SLOT - 1)), chosen, 0.0).astype(BF16)
+    return dot(chosen, held)
+
+
+def add_into(out, base, terms, received):
+    width = terms.shape[1]
+    left = base[:, :width] + terms
+    for r in received:
+        left = left + r[:, :width].astype(F32)
+    out[:, :width] = left.astype(out.dtype)
+    if width < base.shape[1]:
+        right = base[:, width:]
+        for r in received:
+            right = right + r[:, width:].astype(F32)
+        out[:, width:] = right.astype(out.dtype)
+
+
+def fill(base, entry, pieces, out_a, out_b):
+    terms = placed(out_a.shape[0], pieces)
+    cut = out_a.shape[1]
+    add_into(out_a, base[0][entry], terms[:, :cut], [])
+    add_into(out_b, base[1][entry], terms[:, cut:], [])
+
+
+def first_kernel(base_a, base_b, d0, d1, d2, d3, out_a, out_b):
+    fill((base_a, base_b), 0, [d[...] for d in (d0, d1, d2, d3)], out_a, out_b)
+
+
+def next_kernel(base_a, base_b, d0, d1, d2, d3, out_a, out_b):
+    fill((base_a, base_b), 1, [d[...] for d in (d0, d1, d2, d3)], out_a, out_b)
+
+
+def rest_kernel(base_a, base_b, d0, d1, d2, d3, third_a, third_b, own_a, own_b):
+    pieces = [d[...] for d in (d0, d1, d2, d3)]
+    fill((base_a, base_b), 2, [d[0:SLOT] for d in pieces], third_a, third_b)
+    fill((base_a, base_b), 3, [d[SLOT:] for d in pieces], own_a, own_b)
+
+
+def second_kernel(pos, table, first, next_, received, out):
+    own = jnp.where(table[0, pos[0]] == 0, first[...].astype(F32), next_[...])
+    out[...] = (own + received[...].astype(F32)).astype(BF16)
+
+
+def third_kernel(next_, third, from_end, from_middle, inner, outer):
+    for own, received, out in ((next_, from_end, inner), (third, from_middle, outer)):
+        out[...] = (own[...] + received[...].astype(F32)).astype(BF16)
+
+
+def rotated(values, cosine, sine):
+    return (values * cosine + pltpu.roll(values, HD // 2, 1) * sine).astype(BF16)
+
+
+def attended(queries, keys, values, allowed, live):
+    scale = 1.0 / math.sqrt(HD)
+    scores = [
+        jnp.where(allowed, dot(q, k, ((1,), (1,))) * scale, -1e30) for q, k in zip(queries, keys)
+    ]
+    weights = []
+    for v in scores:
+        v = jnp.exp(v - jnp.max(v, axis=1, keepdims=True))
+        weights.append((v / jnp.sum(v, axis=1, keepdims=True)).astype(BF16))
+    return [jnp.where(live, dot(w, v), 0.0).astype(BF16) for w, v in zip(weights, values)]
+
+
+def attend_near_kernel(
+    counts, own, up, down, cosine, sine, out, keys, values, allowed, live, total, queries
+):
+    height, near_cols = out.shape
+    kv_heads = keys.shape[0]
+    kv_cols = kv_heads * HD
+    padded = allowed.shape[0] // (near_cols // HD)
+    total[...] = own[...] + (up[...].astype(F32) + down[...].astype(F32))
+    cos, sin = cosine[...], sine[...]
+    queries[...] = jnp.zeros(queries.shape, BF16)
+    keys[...] = jnp.zeros(keys.shape, BF16)
+    values[...] = jnp.zeros(values.shape, BF16)
+    for k in range(kv_heads):
+        first = near_cols + k * HD
+        values[k, 0:height, :] = total[:, first : first + HD].astype(BF16)
+        first += kv_cols
+        keys[k, 0:height, :] = rotated(total[:, first : first + HD], cos, sin)
+    for g in range(near_cols // HD):
+        head = total[:, g * HD : (g + 1) * HD]
+        queries[g * padded : g * padded + height, :] = rotated(head, cos, sin)
+    t, s = iota((padded, HD), 0), iota((padded, HD), 1)
+    request_t, request_s = over_len(t), over_len(s)
+    limit = jnp.zeros((padded, HD), jnp.int32)
+    row_limit = jnp.zeros((padded, HD), jnp.int32)
+    for r in range(counts.shape[0]):
+        limit = jnp.where(request_s == r, counts[r], limit)
+        row_limit = jnp.where(request_t == r, counts[r], row_limit)
+    here = (request_t == request_s) & (s <= t) & (s - request_s * REQ_LEN < limit)
+    alive = (t - request_t * REQ_LEN) < row_limit
+    for mask, part in ((allowed, here), (live, alive)):
+        mask[...] = jnp.concatenate([part.astype(F32)] * (near_cols // HD), axis=0)
+    (mixed,) = attended(
+        [queries[...]], [keys[kv_heads - 1]], [values[kv_heads - 1]], allowed[...] > 0.5, live[...] > 0.5
+    )
+    for g in range(near_cols // HD):
+        out[:, g * HD : (g + 1) * HD] = mixed[g * padded : g * padded + height]
+
+
+def attend_kernel(
+    own, up, down, near, keys, values, allowed, live, cosine, sine, out, total, queries
+):
+    height, far_cols = own.shape
+    kv_heads = queries.shape[0]
+    group = far_cols // HD // kv_heads
+    padded = queries.shape[1] // group
+    total[...] = own[...] + (up[...].astype(F32) + down[...].astype(F32))
+    cos, sin = cosine[...], sine[...]
+    out[:, far_cols:] = near[...]
+    queries[...] = jnp.zeros(queries.shape, BF16)
+    for k in range(kv_heads):
+        for g in range(group):
+            h = k * group + g
+            head = total[:, h * HD : (h + 1) * HD]
+            queries[k, g * padded : g * padded + height, :] = rotated(head, cos, sin)
+    heads = range(kv_heads)
+    mixed = attended(
+        [queries[k] for k in heads],
+        [keys[k] for k in heads],
+        [values[k] for k in heads],
+        allowed[...] > 0.5,
+        live[...] > 0.5,
+    )
+    for k in heads:
+        for g in range(group):
+            h = k * group + g
+            out[:, h * HD : (h + 1) * HD] = mixed[k][g * padded : g * padded + height]
+
+
+def reduce_body(
+    tokens,
+    w_query,
+    w_keyvalue,
+    adapter_down,
+    adapter_up_query,
+    adapter_up_value,
+    request_adapter,
+    request_tokens,
+    adapter_owner,
+):
+    nz = lax.axis_size("z")
+    z, q, y = lax.axis_index("z"), lax.axis_index("plane"), lax.axis_index("narrow")
+    pos = jnp.stack([z, q, y]).astype(jnp.int32)
+    order = np.array(ORDER, np.int32)
+    inverse = np.zeros((nz, nz), np.int32)
+    for at in range(nz):
+        for shift in range(nz):
+            inverse[at, shift] = ORDER[at].index((at - shift) % nz)
+    order, inverse = jnp.asarray(order), jnp.asarray(inverse)
+    table = jnp.asarray(np.array([SEND2], np.int32))
+    height, width = tokens.shape
+    homes = nz * PLANE
+    requests_here = height // REQ_LEN
+    capacity = 2 * requests_here
+    half = width // 2
+    query_cols, key_cols = w_query.shape[1], w_keyvalue.shape[2]
+    delta_cols = query_cols + key_cols
+    cols = query_cols + 2 * key_cols
+    chunk_cols = cols // 2
+    local_rank = adapter_down.shape[3]
+    shape = jax.ShapeDtypeStruct
+    barrier = lax.optimization_barrier
+    by_c = [(0, 1), (1, 0), (2, 3), (3, 2)]
+    by_x = [(0, 2), (2, 0), (1, 3), (3, 1)]
+    by_xc = [(0, 3), (3, 0), (1, 2), (2, 1)]
+    by_y = [(0, 1), (1, 0)]
+
+    def plane(a, perm):
+        return lax.ppermute(a, "plane", perm)
+
+    pos = jnp.concatenate([pos, request_adapter, adapter_owner])
+    in_hbm = pl.BlockSpec(memory_space=pltpu.HBM)
+    slots = pl.pallas_call(
+        functools.partial(dispatch_kernel, requests_here),
+        out_shape=shape((homes, SLOT, half), BF16),
+        in_specs=[SMEM, VMEM],
+        out_specs=in_hbm,
+        scratch_shapes=[
+            pltpu.VMEM((homes, SLOT, half), BF16),
+            pltpu.SemaphoreType.DMA((homes,)),
+        ],
+        compiler_params=PARAMS,
+        name="dispatch",
+    )(pos, tokens)
+    arrived = lax.all_to_all(slots, ("z", "plane"), 0, 0, tiled=True)
+    q_x = plane(w_query, by_x)
+    w_keyvalue, w_query, _ = barrier((w_keyvalue, w_query, slots))
+    w_kv = w_keyvalue.reshape(w_keyvalue.shape[0], 2 * key_cols)
+    kv_x = plane(w_kv, by_x)
+    down = adapter_down[0].reshape(width, 2 * local_rank)
+
+    packed_rows = capacity * REQ_LEN
+    packed, select, marks = call(
+        compact_kernel,
+        [
+            shape((packed_rows, half), BF16),
+            shape((packed_rows, homes * SLOT), BF16),
+            shape((homes * SLOT, 128), BF16),
+        ],
+        [(pos, SMEM), (order, SMEM), (arrived, VMEM)],
+        name="compact",
+    )
+
+    def rotate_z(a, shift):
+        return lax.ppermute(a, "z", [(i, (i + shift) % nz) for i in range(nz)])
+
+    packed_other = lax.ppermute(packed, "narrow", by_y)
+    tokens, _ = barrier((tokens, packed))
+    slices = call(
+        slices_kernel,
+        [shape((height, width // nz), BF16)] * nz,
+        [(pos, SMEM), (tokens, VMEM)],
+        name="slices",
+    )
+    s1, s2 = rotate_z(slices[1], 1), rotate_z(slices[2], 2)
+    total = call(
+        shrink_kernel,
+        shape((packed_rows, 2 * local_rank), F32),
+        [(pos, SMEM), (packed, VMEM), (down, VMEM)],
+        name="shrink",
+    )
+    packed_other, s1, s2, total, q_x = barrier((packed_other, s1, s2, total, q_x))
+    q_xc = plane(q_x, by_c)
+    shrunk = call(
+        shrink_rest_kernel,
+        shape((packed_rows + SLOT, 2 * local_rank), BF16),
+        [(pos, SMEM), (total, VMEM), (packed_other, VMEM), (down, VMEM)],
+        name="shrink_rest",
+    )
+    shrunk_other = lax.ppermute(shrunk, "narrow", by_y)
+    slices, w_query, w_kv, _ = barrier((slices, w_query, w_kv, shrunk))
+    q_c, kv_c = plane(w_query, by_c), plane(w_kv, by_c)
+    s3 = rotate_z(slices[3], 3)
+    shrunk_other, kv_x = barrier((shrunk_other, kv_x))
+    slices = [slices[0], s1, s2]
+    pieces = call(
+        expand_kernel,
+        [shape((SLOT, delta_cols), BF16)] * (2 * PLANE)
+        + [shape((2 * SLOT, delta_cols), BF16)] * PLANE,
+        [
+            (pos, SMEM),
+            (shrunk, VMEM),
+            (shrunk_other, VMEM),
+            (select, VMEM),
+            (marks, VMEM),
+            (adapter_up_query[0], VMEM),
+            (adapter_up_value[0], VMEM),
+        ],
+        name="expand",
+    )
+
+    def over_plane(four):
+        return [four[0]] + [
+            plane(four[i], perm) for i, perm in ((1, by_c), (2, by_x), (3, by_xc))
+        ]
+
+    first = over_plane(pieces[:PLANE])
+    slices, kv_x, s3, _ = barrier((slices, kv_x, s3, pieces))
+    slices = slices + [s3]
+    kv_xc = plane(kv_x, by_c)
+    padded = -(-height // SLOT) * SLOT
+    base_a, base_b = call(
+        partial_kernel,
+        [shape((nz, height, chunk_cols), F32)] * 2,
+        [(pos, SMEM), (inverse, SMEM)]
+        + [(s, VMEM) for s in slices]
+        + [(w, VMEM) for w in (w_query, q_c, q_x, q_xc, w_kv, kv_c, kv_x, kv_xc)],
+        flops=2 * nz * height * width // nz * cols,
+        nbytes=16 * 2**20,
+        scratch=[pltpu.VMEM((nz * (-(-height // 8) * 8), width // nz), BF16)],
+        name="partial",
+    )
+    block = shape((height, chunk_cols), BF16)
+    wide_block = shape((height, chunk_cols), F32)
+    bases = [(base_a, VMEM), (base_b, VMEM)]
+
+    def of(four):
+        return [(p, VMEM) for p in four]
+
+    sent = call(first_kernel, [block, block], bases + of(first), name="reduce_first")
+    received = [lax.ppermute(s, "z", INWARD) for s in sent]
+    pieces, _ = barrier((pieces, sent))
+    next_ = over_plane(pieces[PLANE : 2 * PLANE])
+    rest = over_plane(pieces[2 * PLANE :])
+    second = call(next_kernel, [wide_block] * 2, bases + of(next_), name="reduce_next")
+    received[0], rest = barrier((received[0], rest))
+    *third, own_a, own_b = call(rest_kernel, [wide_block] * 4, bases + of(rest), name="reduce_rest")
+    scalars = [(pos, SMEM), (table, SMEM)]
+    ends, middles = [], []
+    for chunk in range(2):
+        out = call(
+            second_kernel,
+            block,
+            scalars + of([sent[chunk], second[chunk], received[chunk]]),
+            name="reduce_second",
+        )
+        middles.append(lax.ppermute(out, "z", MIDDLE))
+        ends.append(lax.ppermute(out, "z", INWARD))
+    for chunk in range(2):
+        inner, outer = call(
+            third_kernel,
+            [block, block],
+            of([second[chunk], third[chunk], ends[chunk], middles[chunk]]),
+            name="reduce_third",
+        )
+        middles[chunk] = lax.ppermute(inner, "z", MIDDLE)
+        ends[chunk] = lax.ppermute(outer, "z", PAIRS)
+
+    angles = np.arange(REQ_LEN)[:, None] * (rope_theta ** (-np.arange(HD // 2) * (2.0 / HD)))[None, :]
+    cosine = np.tile(np.concatenate([np.cos(angles)] * 2, axis=1), (requests_here, 1))
+    sine = np.tile(np.concatenate([-np.sin(angles), np.sin(angles)], axis=1), (requests_here, 1))
+    tables = [(jnp.asarray(a.astype(np.float32)), VMEM) for a in (cosine, sine)]
+    near_cols = query_cols - chunk_cols
+    group_rows = query_cols // key_cols * padded
+    key_heads = key_cols // HD
+    held = shape((key_heads, HD, HD), BF16)
+    mask = shape((group_rows, HD), F32)
+    near = call(
+        attend_near_kernel,
+        [shape((height, near_cols), BF16), held, held, mask, mask],
+        [(request_tokens, SMEM)] + of([own_b, ends[1], middles[1]]) + tables,
+        nbytes=8 * 2**20,
+        scratch=[pltpu.VMEM((height, chunk_cols), F32), pltpu.VMEM((group_rows, HD), BF16)],
+        name="attend_near",
+    )
+    return call(
+        attend_kernel,
+        shape((height, query_cols), BF16),
+        of([own_a, ends[0], middles[0], *near]) + tables,
+        scratch=[
+            pltpu.VMEM((height, chunk_cols), F32),
+            pltpu.VMEM((key_heads - 1, group_rows, HD), BF16),
+        ],
+        name="attend",
+    )
+
+
 def solution(mesh):
+    wide, narrow = mesh.shape["wide"], mesh.shape["narrow"]
+    if wide == 4 * PLANE and narrow == 2:
+        grid = Mesh(mesh.devices.reshape(wide // PLANE, PLANE, narrow), ("z", "plane", "narrow"))
+        body, on, over = reduce_body, grid, ("z", "plane")
+    else:
+        body, on, over = gather_body, mesh, "wide"
     return jax.shard_map(
         body,
-        mesh=mesh,
+        mesh=on,
         in_specs=(
-            P("wide", None),
-            P("wide", "narrow"),
-            P("wide", None, "narrow"),
-            P("wide", None, None, "narrow"),
-            P("wide", None, "narrow"),
-            P("wide", None, "narrow"),
-            P("wide"),
-            P("wide"),
+            P(over, None),
+            P(over, "narrow"),
+            P(over, None, "narrow"),
+            P(over, None, None, "narrow"),
+            P(over, None, "narrow"),
+            P(over, None, "narrow"),
+            P(over),
+            P(over),
             P(),
         ),
-        out_specs=P("wide", "narrow"),
+        out_specs=P(over, "narrow"),
         check_vma=False,
     )

time: 325 us -> 114 us (0.35)
  waiting for transfers between devices: 226 us -> 41.3 us
  starting transfers between devices: 16.9 us -> 49.4 us
  local copies, waits for them, and re-layouts: 31.8 us -> 4.92 us
  matrix products: 26.5 us -> 0 us
  Pallas kernels: 0 us -> 17.5 us
  between operations: 13.4 us -> 0.35 us
  blocking collectives: 6.93 us -> 0 us
  other arithmetic: 3.44 us -> 0 us
    all_gather x3 -> x0, waiting for transfers between devices: 156 us -> none  [the longest x1 112 us: body(): query_piece = lax.all_gather(w_query, 'wide', axis=0, tiled=True)]
    all_to_all x3 -> x1, waiting for transfers between devices: 68.1 us -> 21 us  [reduce_body(): arrived = lax.all_to_all(slots, ('z', 'plane'), 0, 0, tiled=True)]
    ppermute x0 -> x30, starting transfers between devices: none -> 41.9 us  [the longest x15 11.8 us: plane(): return lax.ppermute(a, 'plane', perm)]
    dot_general x11 -> x0, matrix products: 25.3 us -> none  [the longest x1 9.44 us: body(): query_sum = jnp.dot(tokens, query_piece, preferred_element_type=jnp.float32)]
    ppermute x0 -> x30, waiting for transfers between devices: none -> 20.3 us  [the longest x3 5.83 us: rotate_z(): return lax.ppermute(a, 'z', [(i, (i + shift) % nz) for i in range(nz)])]
    pallas_call x0 -> x16, Pallas kernels: none -> 17.5 us  [the longest x15 15.7 us: call(): pl.pallas_call(kernel, out_shape=out_shape, in_specs=specs, out_specs=[VM...]
    unnamed x14 -> x26, local copies, waits for them, and re-layouts: 14.6 us -> 4.16 us
    all_to_all x3 -> x1, starting transfers between devices: 16.8 us -> 7.5 us  [reduce_body(): arrived = lax.all_to_all(slots, ('z', 'plane'), 0, 0, tiled=True)]
  transfers between devices with their start and end apart: 6 -> 31, of which waited for: 6 -> 10; matrix products, arithmetic and copies ran while one was open for 12% -> 3% of each run, Pallas kernels for 0% -> 12%
where the time goes in v1:
time: 114 us; the launch traced here: 113 us
  starting transfers between devices  49.4 us (43%)
  waiting for transfers between devices  41.3 us (36%)
  Pallas kernels  17.5 us (15%)
  local copies, waits for them, and re-layouts  4.92 us (4%)
    all_to_all x1, waiting for transfers between devices, reduce_body(): arrived = lax.all_to_all(slots, ('z', 'plane'), 0, 0, tiled=True)  21 us
    pallas_call x15, Pallas kernels, call(): pl.pallas_call(kernel, out_shape=out_shape, in_specs=specs, out_specs=[VM...  15.7 us
    ppermute x15, starting transfers between devices, plane(): return lax.ppermute(a, 'plane', perm)  11.8 us
    ppermute x3, starting transfers between devices, rotate_z(): return lax.ppermute(a, 'z', [(i, (i + shift) % nz) for i in range(nz)])  8.61 us
    all_to_all x1, starting transfers between devices, reduce_body(): arrived = lax.all_to_all(slots, ('z', 'plane'), 0, 0, tiled=True)  7.5 us
    ppermute x2, starting transfers between devices, reduce_body(): ends[chunk] = lax.ppermute(outer, 'z', PAIRS)  6.19 us
    ppermute x3, waiting for transfers between devices, rotate_z(): return lax.ppermute(a, 'z', [(i, (i + shift) % nz) for i in range(nz)])  5.83 us
    ppermute x2, starting transfers between devices, reduce_body(): received = [lax.ppermute(s, 'z', INWARD) for s in sent]  5.57 us
  transfers between devices with their start and end apart: 31, of which 10 were waited for; matrix products, arithmetic and copies ran while one was open for 3% of the time, Pallas kernels for 12%

profile of v1, /device:TPU:0, one launch (start us, length us, event | category | flops | bytes accessed | tf_op | source)
XLA Modules:
  0.0 113.4 jit_solution(13711118188965341184)
XLA Ops:
  0.0 0.8 concatenate.3.pos
  0.8 1.1 copy-done
  1.9 1.8 %dispatch.1 = bf16[16,16,2048]{2,1,0:T(8,128)(2,1)} custom-call(s32[25]{0:T(128)S(1)} %concatenate.3.pos, bf16[84,4096]{1,0:T(8,128)(2,1)S(1)} %copy-done), custom_call_target="tpu_custom_call" | custom-call | tf_op jit(solution)/shard_map/dispatch/pallas_call | solution.py:498
  3.7 7.5 %all-to-all-start = ((bf16[16,16,2048]{2,1,0:T(8,128)(2,1)}), bf16[16,16,2048]{2,1,0:T(8,128)(2,1)S(1)}, u32[]{:S(2)}, u32[]{:S(2)}) async-start(bf16[16,16,2048]{2,1,0:T(8,128)(2,1)} %dispatch.1), calls=%async_computation | async-start | bytes 2097152 | tf_op jit(solution)/shard_map/all_to_all | solution.py:510
  11.2 2.0 %collective-permute-start.3 = (bf16[256,2048]{1,0:T(8,128)(2,1)S(1)}, bf16[256,2048]{1,0:T(8,128)(2,1)}, u32[]{:S(2)}, u32[]{:S(2)}) collective-permute-start(bf16[256,2048]{1,0:T(8,128)(2,1)S(1)} %copy-done.9), channel_id=1, source_target_pairs={{0,4},{4,0},{2,6},{6,2},{1,5},{5,1},{3,7},{7,3},{8,12},{12,8},{10,... | collective-permute-start | bytes 3145736 | tf_op jit(solution)/shard_map/ppermute | solution.py:494
  13.2 21.0 %all-to-all-done.arrived = bf16[16,16,2048]{2,1,0:T(8,128)(2,1)S(1)} async-done(((bf16[16,16,2048]{2,1,0:T(8,128)(2,1)}), bf16[16,16,2048]{2,1,0:T(8,128)(2,1)S(1)}, u32[]{:S(2)}, u32[]{:S(2)}) %all-to-all-start) | async-done | bytes 1048608 | tf_op jit(solution)/shard_map/all_to_all | solution.py:510
  34.2 1.2 %compact.1 = (bf16[168,2048]{1,0:T(8,128)(2,1)S(1)}, bf16[168,256]{1,0:T(8,128)(2,1)S(1)}, bf16[256,128]{1,0:T(8,128)(2,1)S(1)}) custom-call(s32[25]{0:T(128)S(1)} %concatenate.3.pos, s32[4,4]{1,0:T(4,128)S(1)} %copy-done.6, bf16[16,16,2048]{2,1,0:T(8,128)(2,1)S(1)} %all-to-all-done.arrived), custom_call_target="tpu_custom_call" | custom-call | tf_op jit(solution)/shard_map/compact/pallas_call | solution.py:167
  35.4 1.6 %collective-permute-start = (bf16[168,2048]{1,0:T(8,128)(2,1)S(1)}, bf16[168,2048]{1,0:T(8,128)(2,1)S(1)}, u32[]{:S(2)}, u32[]{:S(2)}) collective-permute-start(bf16[168,2048]{1,0:T(8,128)(2,1)S(1)} %get-tuple-element.75.own), channel_id=1, source_target_pairs={{0,1},{1,0},{2,3},{3,2},{4,5},{5,4},{6,7},{7,6},{8,9},{9,8},{10,11... | collective-permute-start | bytes 2064392 | tf_op jit(solution)/shard_map/ppermute | solution.py:532
  37.0 0.6 slices.1
  37.7 3.3 %collective-permute-start.1 = (bf16[84,1024]{1,0:T(8,128)(2,1)S(1)}, bf16[84,1024]{1,0:T(8,128)(2,1)S(1)}, u32[]{:S(2)}, u32[]{:S(2)}) collective-permute-start(bf16[84,1024]{1,0:T(8,128)(2,1)S(1)} %get-tuple-element.78), channel_id=1, source_target_pairs={{0,8},{8,16},{16,24},{24,0},{1,9},{9,17},{17,25},{25,1},{2,10},{10... | collective-permute-start | bytes 516104 | tf_op jit(solution)/shard_map/ppermute | solution.py:530
  41.0 1.9 %collective-permute-start.2 = (bf16[84,1024]{1,0:T(8,128)(2,1)S(1)}, bf16[84,1024]{1,0:T(8,128)(2,1)S(1)}, u32[]{:S(2)}, u32[]{:S(2)}) collective-permute-start(bf16[84,1024]{1,0:T(8,128)(2,1)S(1)} %get-tuple-element.79), channel_id=1, source_target_pairs={{0,16},{8,24},{16,0},{24,8},{1,17},{9,25},{17,1},{25,9},{2,18},{10... | collective-permute-start | bytes 516104 | tf_op jit(solution)/shard_map/ppermute | solution.py:530
  42.9 0.1 copy.15
  43.0 1.6 %collective-permute-start.5 = (bf16[256,1024]{1,0:T(8,128)(2,1)S(1)}, bf16[256,1024]{1,0:T(8,128)(2,1)S(1)}, u32[]{:S(2)}, u32[]{:S(2)}) collective-permute-start(bf16[256,1024]{1,0:T(8,128)(2,1)S(1)} %bitcast.13), channel_id=1, source_target_pairs={{0,4},{4,0},{2,6},{6,2},{1,5},{5,1},{3,7},{7,3},{8,12},{12,8},{10,... | collective-permute-start | bytes 1572872 | tf_op jit(solution)/shard_map/ppermute | solution.py:494
  44.5 2.9 %copy.16 = bf16[512,8,2,256]{3,1,2,0:T(8,128)(2,1)S(1)} copy(bf16[512,8,2,256]{3,2,1,0:T(2,128)(2,1)} %bitcast.17) | data formatting | bytes 8388608
  47.5 1.1 shrink.1.total
  48.6 0.0 collective-permute-done.3.q2
  48.6 5.4 %collective-permute-done.2.s2 = bf16[84,1024]{1,0:T(8,128)(2,1)S(1)} collective-permute-done((bf16[84,1024]{1,0:T(8,128)(2,1)S(1)}, bf16[84,1024]{1,0:T(8,128)(2,1)S(1)}, u32[]{:S(2)}, u32[]{:S(2)}) %collective-permute-start.2) | collective-permute-done | bytes 172064 | tf_op jit(solution)/shard_map/ppermute | solution.py:530
  54.0 1.1 shrink_rest.1.own
  55.1 0.0 copy-start.10
  55.1 0.1 collective-permute-start.7
  55.2 0.5 collective-permute-start.8
  55.7 0.9 collective-permute-start.4
  56.6 3.4 %collective-permute-start.6 = (bf16[84,1024]{1,0:T(8,128)(2,1)S(1)}, bf16[84,1024]{1,0:T(8,128)(2,1)S(1)}, u32[]{:S(2)}, u32[]{:S(2)}) collective-permute-start(bf16[84,1024]{1,0:T(8,128)(2,1)S(1)} %get-tuple-element.89), channel_id=1, source_target_pairs={{0,24},{8,0},{16,8},{24,16},{1,25},{9,1},{17,9},{25,17},{2,26},{10... | collective-permute-start | bytes 516104 | tf_op jit(solution)/shard_map/ppermute | solution.py:530
  60.0 2.4 %collective-permute-done.4.other = bf16[184,512]{1,0:T(8,128)(2,1)S(1)} collective-permute-done((bf16[184,512]{1,0:T(8,128)(2,1)S(1)}, bf16[184,512]{1,0:T(8,128)(2,1)S(1)}, u32[]{:S(2)}, u32[]{:S(2)}) %collective-permute-start.4) | collective-permute-done | bytes 188448 | tf_op jit(solution)/shard_map/ppermute | solution.py:555
  62.4 1.6 %expand.1 = (bf16[16,2560]{1,0:T(8,128)(2,1)S(1)}, bf16[16,2560]{1,0:T(8,128)(2,1)S(1)}, bf16[16,2560]{1,0:T(8,128)(2,1)S(1)}, bf16[16,2560]{1,0:T(8,128)(2,1)S(...) custom-call(s32[25]{0:T(128)S(1)} %concatenate.3.pos, ...), custom_call_target="tpu_custom_call" | custom-call | tf_op jit(solution)/shard_map/expand/pallas_call | solution.py:167
  64.0 0.5 collective-permute-done.6.s3
  64.5 0.5 collective-permute-start.11
  65.0 1.9 %collective-permute-start.12 = (bf16[16,2560]{1,0:T(8,128)(2,1)S(1)}, bf16[16,2560]{1,0:T(8,128)(2,1)S(1)}, u32[]{:S(2)}, u32[]{:S(2)}) collective-permute-start(bf16[16,2560]{1,0:T(8,128)(2,1)S(1)} %get-tuple-element.95), channel_id=1, source_target_pairs={{0,4},{4,0},{2,6},{6,2},{1,5},{5,1},{3,7},{7,3},{8,12},{12,8},{10,... | collective-permute-start | bytes 245768 | tf_op jit(solution)/shard_map/ppermute | solution.py:494
  66.9 1.1 collective-permute-start.13
  68.1 3.7 %partial.1 = (f32[4,84,1536]{2,1,0:T(8,128)S(1)}, f32[4,84,1536]{2,1,0:T(8,128)S(1)}) custom-call(s32[25]{0:T(128)S(1)} %concatenate.3.pos, s32[4,4]{1,0:T(4,128)S(1)} %copy-done.10, bf16[84,1024]{1,0:T(8,128)(2,1)S(1)} %get-tuple-element.105.s0, bf16[84,1024]{1,0:T(8,128)(2,1)S(1)} %collective-permute-done.1.s1, ...), custom_call_target="tpu_custom_call" | custom-call | flops 2113929216 | bytes 16777216 | tf_op jit(solution)/shard_map/partial/pallas_call | solution.py:167
  71.8 0.6 reduce_first.1
  72.4 4.3 %collective-permute-start.25 = (bf16[84,1536]{1,0:T(8,128)(2,1)S(1)}, bf16[84,1536]{1,0:T(8,128)(2,1)S(1)}, u32[]{:S(2)}, u32[]{:S(2)}) collective-permute-start(bf16[84,1536]{1,0:T(8,128)(2,1)S(1)} %get-tuple-element.116.first), channel_id=1, source_target_pairs={{0,8},{24,16},{1,9},{25,17},{2,10},{26,18},{3,11},{27,19},{4,12},{... | collective-permute-start | bytes 774152 | tf_op jit(solution)/shard_map/ppermute | solution.py:606
  76.6 0.0 copy-start.7
  76.6 1.3 %collective-permute-start.14 = (bf16[84,1536]{1,0:T(8,128)(2,1)S(1)}, bf16[84,1536]{1,0:T(8,128)(2,1)S(1)}, u32[]{:S(2)}, u32[]{:S(2)}) collective-permute-start(bf16[84,1536]{1,0:T(8,128)(2,1)S(1)} %get-tuple-element.115.first), channel_id=1, source_target_pairs={{0,8},{24,16},{1,9},{25,17},{2,10},{26,18},{3,11},{27,19},{4,12},{... | collective-permute-start | bytes 774152 | tf_op jit(solution)/shard_map/ppermute | solution.py:606
  78.0 0.1 collective-permute-start.18
  78.1 1.1 collective-permute-start.19
  79.2 0.8 collective-permute-start.20
  79.9 0.3 collective-permute-start.15
  80.3 3.1 %collective-permute-done.19.d2 = bf16[16,2560]{1,0:T(8,128)(2,1)S(1)} collective-permute-done((bf16[16,2560]{1,0:T(8,128)(2,1)S(1)}, bf16[16,2560]{1,0:T(8,128)(2,1)S(1)}, u32[]{:S(2)}, u32[]{:S(2)}) %collective-permute-start.19) | collective-permute-done | bytes 81952 | tf_op jit(solution)/shard_map/ppermute | solution.py:494
  83.4 1.0 collective-permute-start.16
  84.4 0.7 collective-permute-start.17
  85.1 0.6 reduce_next.1
  85.7 0.7 reduce_second.3
  86.4 2.1 %collective-permute-start.26 = (bf16[84,1536]{1,0:T(8,128)(2,1)S(1)}, bf16[84,1536]{1,0:T(8,128)(2,1)S(1)}, u32[]{:S(2)}, u32[]{:S(2)}) collective-permute-start(bf16[84,1536]{1,0:T(8,128)(2,1)S(1)} %reduce_second.3), channel_id=1, source_target_pairs={{0,8},{24,16},{1,9},{25,17},{2,10},{26,18},{3,11},{27,19},{4,12},{... | collective-permute-start | bytes 774152 | tf_op jit(solution)/shard_map/ppermute | solution.py:623
  88.5 0.7 collective-permute-start.27
  89.2 0.8 collective-permute-done.16.d2
  90.0 0.8 collective-permute-done.17.d3
  90.8 0.6 reduce_second.2
  91.5 2.4 %collective-permute-start.21 = (bf16[84,1536]{1,0:T(8,128)(2,1)S(1)}, bf16[84,1536]{1,0:T(8,128)(2,1)S(1)}, u32[]{:S(2)}, u32[]{:S(2)}) collective-permute-start(bf16[84,1536]{1,0:T(8,128)(2,1)S(1)} %reduce_second.2), channel_id=1, source_target_pairs={{0,8},{24,16},{1,9},{25,17},{2,10},{26,18},{3,11},{27,19},{4,12},{... | collective-permute-start | bytes 774152 | tf_op jit(solution)/shard_map/ppermute | solution.py:623
  93.9 0.7 collective-permute-start.22
  94.6 1.0 reduce_rest.1
  95.5 0.0 copy-start.4
  95.6 0.0 copy-start.5
  95.6 0.1 reduce_third.3
  95.7 2.3 %collective-permute-start.28 = (bf16[84,1536]{1,0:T(8,128)(2,1)S(1)}, bf16[84,1536]{1,0:T(8,128)(2,1)S(1)}, u32[]{:S(2)}, u32[]{:S(2)}) collective-permute-start(bf16[84,1536]{1,0:T(8,128)(2,1)S(1)} %get-tuple-element.138), channel_id=1, source_target_pairs={{0,8},{8,0},{16,24},{24,16},{1,9},{9,1},{17,25},{25,17},{2,10},{10... | collective-permute-start | bytes 774152 | tf_op jit(solution)/shard_map/ppermute | solution.py:632
  98.0 0.7 collective-permute-start.29
  98.7 1.9 %collective-permute-done.21.from_end = bf16[84,1536]{1,0:T(8,128)(2,1)S(1)} collective-permute-done((bf16[84,1536]{1,0:T(8,128)(2,1)S(1)}, bf16[84,1536]{1,0:T(8,128)(2,1)S(1)}, u32[]{:S(2)}, u32[]{:S(2)}) %collective-permute-start.21) | collective-permute-done | bytes 258080 | tf_op jit(solution)/shard_map/ppermute | solution.py:623
  100.7 0.1 reduce_third.2
  100.8 3.9 %collective-permute-start.23 = (bf16[84,1536]{1,0:T(8,128)(2,1)S(1)}, bf16[84,1536]{1,0:T(8,128)(2,1)S(1)}, u32[]{:S(2)}, u32[]{:S(2)}) collective-permute-start(bf16[84,1536]{1,0:T(8,128)(2,1)S(1)} %get-tuple-element.133), channel_id=1, source_target_pairs={{0,8},{8,0},{16,24},{24,16},{1,9},{9,1},{17,25},{25,17},{2,10},{10... | collective-permute-start | bytes 774152 | tf_op jit(solution)/shard_map/ppermute | solution.py:632
  104.6 0.7 collective-permute-start.24
  105.3 1.2 %collective-permute-done.28.up = bf16[84,1536]{1,0:T(8,128)(2,1)S(1)} collective-permute-done((bf16[84,1536]{1,0:T(8,128)(2,1)S(1)}, bf16[84,1536]{1,0:T(8,128)(2,1)S(1)}, u32[]{:S(2)}, u32[]{:S(2)}) %collective-permute-start.28) | collective-permute-done | bytes 258080 | tf_op jit(solution)/shard_map/ppermute | solution.py:632
  106.5 1.2 %attend_near.1 = (bf16[84,512]{1,0:T(8,128)(2,1)S(1)}, bf16[4,128,128]{2,1,0:T(8,128)(2,1)S(1)}, bf16[4,128,128]{2,1,0:T(8,128)(2,1)S(1)}, f32[384,128]{1,0:T(8,128)S(1)}, f32[384,128]{1,0:T(8,128)S(1)}) custom-call(s32[6]{0:T(128)S(1)} %copy-done.8, f32[84,1536]{1,0:T(8,128)S(1)} %get-tuple-element.135.own, ...), custom_call_target="tpu_custom_call" | custom-call | bytes 8388608 | tf_op jit(solution)/shard_map/attend_near/pallas_call | solution.py:167
  107.7 4.2 %collective-permute-done.23.up = bf16[84,1536]{1,0:T(8,128)(2,1)S(1)} collective-permute-done((bf16[84,1536]{1,0:T(8,128)(2,1)S(1)}, bf16[84,1536]{1,0:T(8,128)(2,1)S(1)}, u32[]{:S(2)}, u32[]{:S(2)}) %collective-permute-start.23) | collective-permute-done | bytes 258080 | tf_op jit(solution)/shard_map/ppermute | solution.py:632
  111.8 1.6 %attend.1 = bf16[84,2048]{1,0:T(8,128)(2,1)} custom-call(f32[84,1536]{1,0:T(8,128)S(1)} %get-tuple-element.125.own, bf16[84,1536]{1,0:T(8,128)(2,1)S(1)} %collective-permute-done.23.up, bf16[84,1536]{1,0:T(8,128)(2,1)S(1)} %collective-permute-done.24.down, bf16[84,512]{1,0:T(8,128)(2,1)S(1)} %get-tuple-element.140.near, ...), custom_call_target="tpu_custom_call" | custom-call | tf_op jit(solution)/shard_map/attend/pallas_call | solution.py:167
  (41 shorter events, 0.1 us)
Async XLA Ops:
  0.0 34.2 %copy-start.6 = (s32[4,4]{1,0:T(4,128)S(1)}, s32[4,4]{1,0:T(4,128)}, u32[]{:S(2)}) copy-start(s32[4,4]{1,0:T(4,128)} %constant.21.clone.order) | copy-start | bytes 196
  0.8 1.1 copy-start
  1.9 9.3 %copy-start.9 = (bf16[256,2048]{1,0:T(8,128)(2,1)S(1)}, bf16[256,2048]{1,0:T(8,128)(2,1)}, u32[]{:S(2)}) copy-start(bf16[256,2048]{1,0:T(8,128)(2,1)} %q0) | copy-start | bytes 3145732
  1.9 35.1 %copy-start.1 = (bf16[84,4096]{1,0:T(8,128)(2,1)S(1)}, bf16[84,4096]{1,0:T(8,128)(2,1)}, u32[]{:S(2)}) copy-start(bf16[84,4096]{1,0:T(8,128)(2,1)} %tokens.2) | copy-start | bytes 2064388
  3.7 39.2 %copy-start.11 = (bf16[256,2,512]{2,1,0:T(2,128)(2,1)S(1)}, bf16[256,2,512]{2,1,0:T(2,128)(2,1)}, u32[]{:S(2)}) copy-start(bf16[256,2,512]{2,1,0:T(2,128)(2,1)} %param.16) | copy-start | bytes 1572868
  3.7 30.5 %all-to-all-start = ((bf16[16,16,2048]{2,1,0:T(8,128)(2,1)}), bf16[16,16,2048]{2,1,0:T(8,128)(2,1)S(1)}, u32[]{:S(2)}, u32[]{:S(2)}) async-start(bf16[16,16,2048]{2,1,0:T(8,128)(2,1)} %dispatch.1), calls=%async_computation | async-start | bytes 2097152 | tf_op jit(solution)/shard_map/all_to_all | solution.py:510
  11.2 37.4 %collective-permute-start.3 = (bf16[256,2048]{1,0:T(8,128)(2,1)S(1)}, bf16[256,2048]{1,0:T(8,128)(2,1)}, u32[]{:S(2)}, u32[]{:S(2)}) collective-permute-start(bf16[256,2048]{1,0:T(8,128)(2,1)S(1)} %copy-done.9), channel_id=1, source_target_pairs={{0,4},{4,0},{2,6},{6,2},{1,5},{5,1},{3,7},{7,3},{8,12},{12,8},{10,... | collective-permute-start | bytes 3145736 | tf_op jit(solution)/shard_map/ppermute | solution.py:494
  35.4 18.5 %collective-permute-start = (bf16[168,2048]{1,0:T(8,128)(2,1)S(1)}, bf16[168,2048]{1,0:T(8,128)(2,1)S(1)}, u32[]{:S(2)}, u32[]{:S(2)}) collective-permute-start(bf16[168,2048]{1,0:T(8,128)(2,1)S(1)} %get-tuple-element.75.own), channel_id=1, source_target_pairs={{0,1},{1,0},{2,3},{3,2},{4,5},{5,4},{6,7},{7,6},{8,9},{9,8},{10,11... | collective-permute-start | bytes 2064392 | tf_op jit(solution)/shard_map/ppermute | solution.py:532
  37.7 10.9 %collective-permute-start.1 = (bf16[84,1024]{1,0:T(8,128)(2,1)S(1)}, bf16[84,1024]{1,0:T(8,128)(2,1)S(1)}, u32[]{:S(2)}, u32[]{:S(2)}) collective-permute-start(bf16[84,1024]{1,0:T(8,128)(2,1)S(1)} %get-tuple-element.78), channel_id=1, source_target_pairs={{0,8},{8,16},{16,24},{24,0},{1,9},{9,17},{17,25},{25,1},{2,10},{10... | collective-permute-start | bytes 516104 | tf_op jit(solution)/shard_map/ppermute | solution.py:530
  41.0 13.0 %collective-permute-start.2 = (bf16[84,1024]{1,0:T(8,128)(2,1)S(1)}, bf16[84,1024]{1,0:T(8,128)(2,1)S(1)}, u32[]{:S(2)}, u32[]{:S(2)}) collective-permute-start(bf16[84,1024]{1,0:T(8,128)(2,1)S(1)} %get-tuple-element.79), channel_id=1, source_target_pairs={{0,16},{8,24},{16,0},{24,8},{1,17},{9,25},{17,1},{25,9},{2,18},{10... | collective-permute-start | bytes 516104 | tf_op jit(solution)/shard_map/ppermute | solution.py:530
  43.0 17.0 %collective-permute-start.5 = (bf16[256,1024]{1,0:T(8,128)(2,1)S(1)}, bf16[256,1024]{1,0:T(8,128)(2,1)S(1)}, u32[]{:S(2)}, u32[]{:S(2)}) collective-permute-start(bf16[256,1024]{1,0:T(8,128)(2,1)S(1)} %bitcast.13), channel_id=1, source_target_pairs={{0,4},{4,0},{2,6},{6,2},{1,5},{5,1},{3,7},{7,3},{8,12},{12,8},{10,... | collective-permute-start | bytes 1572872 | tf_op jit(solution)/shard_map/ppermute | solution.py:494
  48.6 13.8 %copy-start.2 = (bf16[1,512,2048]{2,1,0:T(8,128)(2,1)S(1)}, bf16[1,512,2048]{2,1,0:T(8,128)(2,1)}, u32[]{:S(2)}) copy-start(bf16[1,512,2048]{2,1,0:T(8,128)(2,1)} %param.18) | copy-start | bytes 6291460
  48.6 13.8 %copy-start.3 = (bf16[1,512,512]{2,1,0:T(8,128)(2,1)S(1)}, bf16[1,512,512]{2,1,0:T(8,128)(2,1)}, u32[]{:S(2)}) copy-start(bf16[1,512,512]{2,1,0:T(8,128)(2,1)} %param.19) | copy-start | bytes 1572868
  55.1 13.0 %copy-start.10 = (s32[4,4]{1,0:T(4,128)S(1)}, s32[4,4]{1,0:T(4,128)}, u32[]{:S(2)}) copy-start(s32[4,4]{1,0:T(4,128)} %constant.22.clone.inverse) | copy-start | bytes 196
  55.1 13.0 %collective-permute-start.7 = (bf16[256,2048]{1,0:T(8,128)(2,1)S(1)}, bf16[256,2048]{1,0:T(8,128)(2,1)S(1)}, u32[]{:S(2)}, u32[]{:S(2)}) collective-permute-start(bf16[256,2048]{1,0:T(8,128)(2,1)S(1)} %copy-done.9), channel_id=1, source_target_pairs={{0,2},{2,0},{4,6},{6,4},{1,3},{3,1},{5,7},{7,5},{8,10},{10,8},{12,... | collective-permute-start | bytes 3145736 | tf_op jit(solution)/shard_map/ppermute | solution.py:494
  55.2 12.9 %collective-permute-start.8 = (bf16[256,2048]{1,0:T(8,128)(2,1)}, bf16[256,2048]{1,0:T(8,128)(2,1)S(1)}, u32[]{:S(2)}, u32[]{:S(2)}) collective-permute-start(bf16[256,2048]{1,0:T(8,128)(2,1)} %collective-permute-done.3.q2), channel_id=1, source_target_pairs={{0,2},{2,0},{4,6},{6,4},{1,3},{3,1},{5,7},{7,5},{8,10},{10,8},{12,... | collective-permute-start | bytes 3145736 | tf_op jit(solution)/shard_map/ppermute | solution.py:494
  55.7 6.7 %collective-permute-start.4 = (bf16[184,512]{1,0:T(8,128)(2,1)S(1)}, bf16[184,512]{1,0:T(8,128)(2,1)S(1)}, u32[]{:S(2)}, u32[]{:S(2)}) collective-permute-start(bf16[184,512]{1,0:T(8,128)(2,1)S(1)} %shrink_rest.1.own), channel_id=1, source_target_pairs={{0,1},{1,0},{2,3},{3,2},{4,5},{5,4},{6,7},{7,6},{8,9},{9,8},{10,11... | collective-permute-start | bytes 565256 | tf_op jit(solution)/shard_map/ppermute | solution.py:555
  56.6 7.9 %collective-permute-start.6 = (bf16[84,1024]{1,0:T(8,128)(2,1)S(1)}, bf16[84,1024]{1,0:T(8,128)(2,1)S(1)}, u32[]{:S(2)}, u32[]{:S(2)}) collective-permute-start(bf16[84,1024]{1,0:T(8,128)(2,1)S(1)} %get-tuple-element.89), channel_id=1, source_target_pairs={{0,24},{8,0},{16,8},{24,16},{1,25},{9,1},{17,9},{25,17},{2,26},{10... | collective-permute-start | bytes 516104 | tf_op jit(solution)/shard_map/ppermute | solution.py:530
  60.0 5.0 %collective-permute-start.9 = (bf16[256,1024]{1,0:T(8,128)(2,1)S(1)}, bf16[256,1024]{1,0:T(8,128)(2,1)S(1)}, u32[]{:S(2)}, u32[]{:S(2)}) collective-permute-start(bf16[256,1024]{1,0:T(8,128)(2,1)S(1)} %bitcast.14), channel_id=1, source_target_pairs={{0,2},{2,0},{4,6},{6,4},{1,3},{3,1},{5,7},{7,5},{8,10},{10,8},{12,... | collective-permute-start | bytes 1572872 | tf_op jit(solution)/shard_map/ppermute | solution.py:494
  64.5 2.5 %collective-permute-start.10 = (bf16[256,1024]{1,0:T(8,128)(2,1)S(1)}, bf16[256,1024]{1,0:T(8,128)(2,1)S(1)}, u32[]{:S(2)}, u32[]{:S(2)}) collective-permute-start(bf16[256,1024]{1,0:T(8,128)(2,1)S(1)} %collective-permute-done.5.v2), channel_id=1, source_target_pairs={{0,2},{2,0},{4,6},{6,4},{1,3},{3,1},{5,7},{7,5},{8,10},{10,8},{12,... | collective-permute-start | bytes 1572872 | tf_op jit(solution)/shard_map/ppermute | solution.py:494
  64.5 7.3 %collective-permute-start.11 = (bf16[16,2560]{1,0:T(8,128)(2,1)S(1)}, bf16[16,2560]{1,0:T(8,128)(2,1)S(1)}, u32[]{:S(2)}, u32[]{:S(2)}) collective-permute-start(bf16[16,2560]{1,0:T(8,128)(2,1)S(1)} %get-tuple-element.94), channel_id=1, source_target_pairs={{0,2},{2,0},{4,6},{6,4},{1,3},{3,1},{5,7},{7,5},{8,10},{10,8},{12,... | collective-permute-start | bytes 245768 | tf_op jit(solution)/shard_map/ppermute | solution.py:494
  65.0 6.8 %collective-permute-start.12 = (bf16[16,2560]{1,0:T(8,128)(2,1)S(1)}, bf16[16,2560]{1,0:T(8,128)(2,1)S(1)}, u32[]{:S(2)}, u32[]{:S(2)}) collective-permute-start(bf16[16,2560]{1,0:T(8,128)(2,1)S(1)} %get-tuple-element.95), channel_id=1, source_target_pairs={{0,4},{4,0},{2,6},{6,2},{1,5},{5,1},{3,7},{7,3},{8,12},{12,8},{10,... | collective-permute-start | bytes 245768 | tf_op jit(solution)/shard_map/ppermute | solution.py:494
  66.9 4.9 %collective-permute-start.13 = (bf16[16,2560]{1,0:T(8,128)(2,1)S(1)}, bf16[16,2560]{1,0:T(8,128)(2,1)S(1)}, u32[]{:S(2)}, u32[]{:S(2)}) collective-permute-start(bf16[16,2560]{1,0:T(8,128)(2,1)S(1)} %get-tuple-element.96), channel_id=1, source_target_pairs={{0,6},{6,0},{2,4},{4,2},{1,7},{7,1},{3,5},{5,3},{8,14},{14,8},{10,... | collective-permute-start | bytes 245768 | tf_op jit(solution)/shard_map/ppermute | solution.py:494
  72.4 13.3 %collective-permute-start.25 = (bf16[84,1536]{1,0:T(8,128)(2,1)S(1)}, bf16[84,1536]{1,0:T(8,128)(2,1)S(1)}, u32[]{:S(2)}, u32[]{:S(2)}) collective-permute-start(bf16[84,1536]{1,0:T(8,128)(2,1)S(1)} %get-tuple-element.116.first), channel_id=1, source_target_pairs={{0,8},{24,16},{1,9},{25,17},{2,10},{26,18},{3,11},{27,19},{4,12},{... | collective-permute-start | bytes 774152 | tf_op jit(solution)/shard_map/ppermute | solution.py:606
  76.6 9.1 %copy-start.7 = (s32[1,4]{1,0:T(1,128)S(1)}, s32[1,4]{1,0:T(1,128)}, u32[]{:S(2)}) copy-start(s32[1,4]{1,0:T(1,128)} %constant.23.clone.table) | copy-start | bytes 52
  76.6 14.2 %collective-permute-start.14 = (bf16[84,1536]{1,0:T(8,128)(2,1)S(1)}, bf16[84,1536]{1,0:T(8,128)(2,1)S(1)}, u32[]{:S(2)}, u32[]{:S(2)}) collective-permute-start(bf16[84,1536]{1,0:T(8,128)(2,1)S(1)} %get-tuple-element.115.first), channel_id=1, source_target_pairs={{0,8},{24,16},{1,9},{25,17},{2,10},{26,18},{3,11},{27,19},{4,12},{... | collective-permute-start | bytes 774152 | tf_op jit(solution)/shard_map/ppermute | solution.py:606
  78.0 1.9 %collective-permute-start.18 = (bf16[16,2560]{1,0:T(8,128)(2,1)S(1)}, bf16[16,2560]{1,0:T(8,128)(2,1)S(1)}, u32[]{:S(2)}, u32[]{:S(2)}) collective-permute-start(bf16[16,2560]{1,0:T(8,128)(2,1)S(1)} %get-tuple-element.127), channel_id=1, source_target_pairs={{0,2},{2,0},{4,6},{6,4},{1,3},{3,1},{5,7},{7,5},{8,10},{10,8},{12,... | collective-permute-start | bytes 245768 | tf_op jit(solution)/shard_map/ppermute | solution.py:494
  78.1 5.2 %collective-permute-start.19 = (bf16[16,2560]{1,0:T(8,128)(2,1)S(1)}, bf16[16,2560]{1,0:T(8,128)(2,1)S(1)}, u32[]{:S(2)}, u32[]{:S(2)}) collective-permute-start(bf16[16,2560]{1,0:T(8,128)(2,1)S(1)} %get-tuple-element.128), channel_id=1, source_target_pairs={{0,4},{4,0},{2,6},{6,2},{1,5},{5,1},{3,7},{7,3},{8,12},{12,8},{10,... | collective-permute-start | bytes 245768 | tf_op jit(solution)/shard_map/ppermute | solution.py:494
  79.2 5.2 %collective-permute-start.20 = (bf16[16,2560]{1,0:T(8,128)(2,1)S(1)}, bf16[16,2560]{1,0:T(8,128)(2,1)S(1)}, u32[]{:S(2)}, u32[]{:S(2)}) collective-permute-start(bf16[16,2560]{1,0:T(8,128)(2,1)S(1)} %get-tuple-element.129), channel_id=1, source_target_pairs={{0,6},{6,0},{2,4},{4,2},{1,7},{7,1},{3,5},{5,3},{8,14},{14,8},{10,... | collective-permute-start | bytes 245768 | tf_op jit(solution)/shard_map/ppermute | solution.py:494
  79.9 8.6 %collective-permute-start.15 = (bf16[32,2560]{1,0:T(8,128)(2,1)S(1)}, bf16[32,2560]{1,0:T(8,128)(2,1)S(1)}, u32[]{:S(2)}, u32[]{:S(2)}) collective-permute-start(bf16[32,2560]{1,0:T(8,128)(2,1)S(1)} %get-tuple-element.118), channel_id=1, source_target_pairs={{0,2},{2,0},{4,6},{6,4},{1,3},{3,1},{5,7},{7,5},{8,10},{10,8},{12,... | collective-permute-start | bytes 491528 | tf_op jit(solution)/shard_map/ppermute | solution.py:494
  83.4 6.7 %collective-permute-start.16 = (bf16[32,2560]{1,0:T(8,128)(2,1)S(1)}, bf16[32,2560]{1,0:T(8,128)(2,1)S(1)}, u32[]{:S(2)}, u32[]{:S(2)}) collective-permute-start(bf16[32,2560]{1,0:T(8,128)(2,1)S(1)} %get-tuple-element.119), channel_id=1, source_target_pairs={{0,4},{4,0},{2,6},{6,2},{1,5},{5,1},{3,7},{7,3},{8,12},{12,8},{10,... | collective-permute-start | bytes 491528 | tf_op jit(solution)/shard_map/ppermute | solution.py:494
  84.4 6.4 %collective-permute-start.17 = (bf16[32,2560]{1,0:T(8,128)(2,1)S(1)}, bf16[32,2560]{1,0:T(8,128)(2,1)S(1)}, u32[]{:S(2)}, u32[]{:S(2)}) collective-permute-start(bf16[32,2560]{1,0:T(8,128)(2,1)S(1)} %get-tuple-element.120), channel_id=1, source_target_pairs={{0,6},{6,0},{2,4},{4,2},{1,7},{7,1},{3,5},{5,3},{8,14},{14,8},{10,... | collective-permute-start | bytes 491528 | tf_op jit(solution)/shard_map/ppermute | solution.py:494
  86.4 9.2 %collective-permute-start.26 = (bf16[84,1536]{1,0:T(8,128)(2,1)S(1)}, bf16[84,1536]{1,0:T(8,128)(2,1)S(1)}, u32[]{:S(2)}, u32[]{:S(2)}) collective-permute-start(bf16[84,1536]{1,0:T(8,128)(2,1)S(1)} %reduce_second.3), channel_id=1, source_target_pairs={{0,8},{24,16},{1,9},{25,17},{2,10},{26,18},{3,11},{27,19},{4,12},{... | collective-permute-start | bytes 774152 | tf_op jit(solution)/shard_map/ppermute | solution.py:623
  88.5 7.1 %collective-permute-start.27 = (bf16[84,1536]{1,0:T(8,128)(2,1)S(1)}, bf16[84,1536]{1,0:T(8,128)(2,1)S(1)}, u32[]{:S(2)}, u32[]{:S(2)}) collective-permute-start(bf16[84,1536]{1,0:T(8,128)(2,1)S(1)} %reduce_second.3), channel_id=1, source_target_pairs={{8,16},{16,8},{9,17},{17,9},{10,18},{18,10},{11,19},{19,11},{12,20... | collective-permute-start | bytes 774152 | tf_op jit(solution)/shard_map/ppermute | solution.py:622
  91.5 9.2 %collective-permute-start.21 = (bf16[84,1536]{1,0:T(8,128)(2,1)S(1)}, bf16[84,1536]{1,0:T(8,128)(2,1)S(1)}, u32[]{:S(2)}, u32[]{:S(2)}) collective-permute-start(bf16[84,1536]{1,0:T(8,128)(2,1)S(1)} %reduce_second.2), channel_id=1, source_target_pairs={{0,8},{24,16},{1,9},{25,17},{2,10},{26,18},{3,11},{27,19},{4,12},{... | collective-permute-start | bytes 774152 | tf_op jit(solution)/shard_map/ppermute | solution.py:623
  93.9 6.8 %collective-permute-start.22 = (bf16[84,1536]{1,0:T(8,128)(2,1)S(1)}, bf16[84,1536]{1,0:T(8,128)(2,1)S(1)}, u32[]{:S(2)}, u32[]{:S(2)}) collective-permute-start(bf16[84,1536]{1,0:T(8,128)(2,1)S(1)} %reduce_second.2), channel_id=1, source_target_pairs={{8,16},{16,8},{9,17},{17,9},{10,18},{18,10},{11,19},{19,11},{12,20... | collective-permute-start | bytes 774152 | tf_op jit(solution)/shard_map/ppermute | solution.py:622
  95.5 10.9 %copy-start.4 = (f32[84,128]{1,0:T(8,128)S(1)}, f32[84,128]{1,0:T(8,128)}, u32[]{:S(2)}) copy-start(f32[84,128]{1,0:T(8,128)} %constant.24.clone.cosine) | copy-start | bytes 129028
  95.6 10.9 %copy-start.5 = (f32[84,128]{1,0:T(8,128)S(1)}, f32[84,128]{1,0:T(8,128)}, u32[]{:S(2)}) copy-start(f32[84,128]{1,0:T(8,128)} %constant.25.clone.sine) | copy-start | bytes 129028
  95.6 10.9 %copy-start.8 = (s32[6]{0:T(128)S(1)}, s32[6]{0:T(128)}, u32[]{:S(2)}) copy-start(s32[6]{0:T(128)} %counts.1) | copy-start | bytes 76
  95.7 10.7 %collective-permute-start.28 = (bf16[84,1536]{1,0:T(8,128)(2,1)S(1)}, bf16[84,1536]{1,0:T(8,128)(2,1)S(1)}, u32[]{:S(2)}, u32[]{:S(2)}) collective-permute-start(bf16[84,1536]{1,0:T(8,128)(2,1)S(1)} %get-tuple-element.138), channel_id=1, source_target_pairs={{0,8},{8,0},{16,24},{24,16},{1,9},{9,1},{17,25},{25,17},{2,10},{10... | collective-permute-start | bytes 774152 | tf_op jit(solution)/shard_map/ppermute | solution.py:632
  98.0 8.4 %collective-permute-start.29 = (bf16[84,1536]{1,0:T(8,128)(2,1)S(1)}, bf16[84,1536]{1,0:T(8,128)(2,1)S(1)}, u32[]{:S(2)}, u32[]{:S(2)}) collective-permute-start(bf16[84,1536]{1,0:T(8,128)(2,1)S(1)} %get-tuple-element.139), channel_id=1, source_target_pairs={{8,16},{16,8},{9,17},{17,9},{10,18},{18,10},{11,19},{19,11},{12,20... | collective-permute-start | bytes 774152 | tf_op jit(solution)/shard_map/ppermute | solution.py:631
  100.8 11.1 %collective-permute-start.23 = (bf16[84,1536]{1,0:T(8,128)(2,1)S(1)}, bf16[84,1536]{1,0:T(8,128)(2,1)S(1)}, u32[]{:S(2)}, u32[]{:S(2)}) collective-permute-start(bf16[84,1536]{1,0:T(8,128)(2,1)S(1)} %get-tuple-element.133), channel_id=1, source_target_pairs={{0,8},{8,0},{16,24},{24,16},{1,9},{9,1},{17,25},{25,17},{2,10},{10... | collective-permute-start | bytes 774152 | tf_op jit(solution)/shard_map/ppermute | solution.py:632
  104.6 7.2 %collective-permute-start.24 = (bf16[84,1536]{1,0:T(8,128)(2,1)S(1)}, bf16[84,1536]{1,0:T(8,128)(2,1)S(1)}, u32[]{:S(2)}, u32[]{:S(2)}) collective-permute-start(bf16[84,1536]{1,0:T(8,128)(2,1)S(1)} %get-tuple-element.134), channel_id=1, source_target_pairs={{8,16},{16,8},{9,17},{17,9},{10,18},{18,10},{11,19},{19,11},{12,20... | collective-permute-start | bytes 774152 | tf_op jit(solution)/shard_map/ppermute | solution.py:631

commit v2 on v1

--- a/solution.py
+++ b/solution.py
@@ -188,15 +188,29 @@
     return lax.dot_general(a, b, (contract, ((), ())), preferred_element_type=F32)
 
 
+def owner_of(pos, requests_here, r):
+    return pos[3 + requests_here + pos[3 + r]]
+
+
 def dispatch_kernel(requests_here, pos, tokens, slots, filled, sems):
-    count, _, half = filled.shape
-    columns = pl.ds(pl.multiple_of(pos[2] * half, half), half)
+    count, _, main = filled.shape
+    half = main * SLOT // REQ_LEN
+    tail = half - main
+    height = tokens.shape[0]
+    first = pl.multiple_of(pos[2] * half, half)
     filled[...] = jnp.zeros(filled.shape, filled.dtype)
+    tails = tokens[:, pl.ds(pl.multiple_of(first + main, 128), tail)]
+    packed = 2 * requests_here
+    target, source = iota((packed, height), 0), iota((packed, height), 1)
+    parts = []
+    for j in range(REQ_LEN // 2):
+        pick = (source == target * (REQ_LEN // 2) + j).astype(F32).astype(BF16)
+        parts.append(dot(pick, tails).astype(BF16))
     for r in range(requests_here):
-        owner = pos[3 + requests_here + pos[3 + r]]
-        filled[owner, 0:REQ_LEN, :] = tokens[r * REQ_LEN : (r + 1) * REQ_LEN, columns]
-        mark = (iota((SLOT - REQ_LEN, 128), 0) == 0) & (iota((SLOT - REQ_LEN, 128), 1) == r)
-        filled[owner, REQ_LEN:SLOT, 0:128] = mark.astype(F32).astype(BF16)
+        owner = owner_of(pos, requests_here, r)
+        filled[owner, 0:REQ_LEN, :] = tokens[r * REQ_LEN : (r + 1) * REQ_LEN, pl.ds(first, main)]
+        for j, part in enumerate(parts):
+            filled[owner, REQ_LEN:SLOT, j * tail : (j + 1) * tail] = part[2 * r : 2 * r + 2]
     copies = [
         pltpu.make_async_copy(filled.at[n], slots.at[n], sems.at[n]) for n in range(count)
     ]
@@ -206,44 +220,62 @@
         copy.wait()
 
 
-def slices_kernel(pos, tokens, *slices):
+def slices_kernel(requests_here, pos, tokens, *slices):
     z, q = pos[0], pos[1]
     count = len(slices)
+    height = tokens.shape[0]
     depth = slices[0].shape[1] // PLANE
+    spare = slices[0].shape[0] - height
+    lane = iota((spare, 128), 1)
+    owners = jnp.zeros((spare, 128), F32)
+    for r in range(requests_here):
+        owner = owner_of(pos, requests_here, r).astype(F32)
+        owners = jnp.where(lane == r, owner, owners)
     for shift, out in enumerate(slices):
         to = (z + shift) & (count - 1)
         for i in range(PLANE):
             start = pl.multiple_of((to * PLANE + (q ^ i)) * depth, depth)
-            out[:, i * depth : (i + 1) * depth] = tokens[:, pl.ds(start, depth)]
-
-
-def compact_kernel(pos, order, arrived, packed, select, marks):
+            out[0:height, i * depth : (i + 1) * depth] = tokens[:, pl.ds(start, depth)]
+        out[height:, :] = jnp.zeros((spare, out.shape[1]), BF16)
+        out[height:, 0:128] = owners.astype(BF16)
+
+
+def compact_kernel(pos, order, arrived, packed, select):
     z, q = pos[0], pos[1]
-    count = arrived.shape[0]
+    count, _, main = arrived.shape
     rows = count * SLOT
     blocks = []
     for o in range(count):
         home = order[z, o // PLANE] * PLANE + (q ^ (o % PLANE))
         blocks.append(arrived[home])
     held = jnp.concatenate(blocks, axis=0)
-    here = (iota((rows, 128), 0) & (SLOT - 1)) == REQ_LEN
-    marked = jnp.where(here, held[:, :128].astype(F32), 0.0)
-    marked = jnp.where(iota((rows, 128), 1) < 8, marked, 0.0).astype(BF16)
-    marks[...] = marked
+    top = jnp.zeros((rows, 128), F32)
+    for c in range(main // 128):
+        top = jnp.maximum(top, jnp.abs(held[:, c * 128 : (c + 1) * 128].astype(F32)))
+    used = (top > 0.0).astype(F32).astype(BF16)
     row, col = iota((rows, rows), 0), iota((rows, rows), 1)
     same = ((row >> 4) == (col >> 4)).astype(F32).astype(BF16)
-    which = dot(marked, same, ((0,), (0,)))
-    present = jnp.sum(which, axis=0, keepdims=True)
+    present = jnp.sum(dot(used, same, ((0,), (0,))), axis=0, keepdims=True)
+    present = (present > 0.5).astype(F32)
     earlier = (((row & (SLOT - 1)) == 0) & ((row >> 4) < (col >> 4))).astype(F32).astype(BF16)
     rank = dot(jnp.broadcast_to(present, (8, rows)).astype(BF16), earlier)[:1]
     out_rows = packed.shape[0]
     k = over_len(iota((out_rows, rows), 0))
     place = iota((out_rows, rows), 0) - k * REQ_LEN
-    chosen = (k.astype(F32) == rank) & (present > 0.5)
-    chosen = chosen & (place == (iota((out_rows, rows), 1) & (SLOT - 1)))
-    chosen = chosen.astype(F32).astype(BF16)
+    at = iota((out_rows, rows), 1) & (SLOT - 1)
+    here = (k.astype(F32) == rank) & (present > 0.5)
+    chosen = (here & (place == at)).astype(F32).astype(BF16)
     select[...] = chosen
-    packed[...] = dot(chosen, held).astype(BF16)
+    packed[:, :main] = dot(chosen, held).astype(BF16)
+    tail = packed.shape[1] - main
+    second = (place >= REQ_LEN // 2).astype(jnp.int32)
+    turn = place - second * (REQ_LEN // 2)
+    here = here & (at == REQ_LEN + second)
+    total = jnp.zeros((out_rows, tail), F32)
+    for j in range(REQ_LEN // 2):
+        chosen = (here & (turn == j)).astype(F32).astype(BF16)
+        total += dot(chosen, held[:, j * tail : (j + 1) * tail])
+    packed[:, main:] = total.astype(BF16)
 
 
 def shrink_kernel(pos, own, down, total):
@@ -260,7 +292,7 @@
     out[0:rows, :] = (total[...] + dot(other[...], down[theirs, :])).astype(BF16)
 
 
-def expand_kernel(pos, own, other, select, marks, up_query, up_value, *outs):
+def expand_kernel(pos, own, other, select, up_query, up_value, *outs):
     y = pos[2]
     rank = own.shape[1] // 2
     mine = pl.ds(pl.multiple_of(y * rank, rank), rank)
@@ -273,9 +305,6 @@
     for name, up, first in ((0, up_query, 0), (1, up_value, query_cols)):
         span = slice(name * rank, (name + 1) * rank)
         delta = dot(own_rows[:, span], up[mine, :]) + dot(other_rows[:, span], up[theirs, :])
-        if name == 0:
-            head = delta[:, :128] + marks[...].astype(F32)
-            delta = jnp.concatenate([head, delta[:, 128:]], axis=1)
         delta = delta.astype(BF16)
         for i in range(PLANE):
             for b in range(4):
@@ -286,13 +315,14 @@
                 out[at : at + SLOT, first : first + up.shape[1]] = piece
 
 
-def partial_kernel(pos, inverse, s0, s1, s2, s3, q0, q1, q2, q3, v0, v1, v2, v3, out_a, out_b, rows):
+def partial_kernel(pos, inverse, s0, s1, s2, s3, q0, q1, q2, q3, v0, v1, v2, v3, out_a, out_b, owners, rows):
     z = pos[0]
     count, height, _ = out_a.shape
     padded = rows.shape[0] // count
-    rows[...] = jnp.zeros(rows.shape, rows.dtype)
+    owners[...] = jnp.zeros(owners.shape, owners.dtype)
     for shift, s in enumerate((s0, s1, s2, s3)):
-        rows[shift * padded : shift * padded + height, :] = s[...]
+        rows[shift * padded : (shift + 1) * padded, :] = s[...]
+        owners[inverse[z, shift], 0 : padded - height, :] = s[height:, 0:128]
     tile = 512
     queries, values = (q0, q1, q2, q3), (v0, v1, v2, v3)
     spans = [(queries, n * tile) for n in range(q0.shape[1] // tile)]
@@ -309,19 +339,17 @@
             out[inverse[z, shift], :, at : at + tile] = block
 
 
-def placed(height, pieces):
+def placed(height, pieces, owners, pos):
     held = jnp.concatenate(pieces, axis=0)
     rows = held.shape[0]
-    here = (iota((rows, 128), 0) & (SLOT - 1)) == REQ_LEN
-    marked = jnp.where(here, held[:, :128].astype(F32), 0.0).astype(BF16)
-    same = ((iota((rows, rows), 0) >> 4) == (iota((rows, rows), 1) >> 4)).astype(F32).astype(BF16)
-    which = dot(marked, same, ((0,), (0,))).astype(BF16)
     request = over_len(iota((height, 128), 0))
-    chosen = dot((request == iota((height, 128), 1)).astype(F32).astype(BF16), which)
-    t = iota((height, rows), 0)
+    mine = (request == iota((height, 128), 1)).astype(F32).astype(BF16)
+    owner = dot(mine, owners, ((1,), (1,)))[:, 0:1]
+    t, slot = iota((height, rows), 0), iota((height, rows), 1)
     place = t - over_len(t) * REQ_LEN
-    chosen = jnp.where(place == (iota((height, rows), 1) & (SLOT - 1)), chosen, 0.0).astype(BF16)
-    return dot(chosen, held)
+    sender = (pos[0] * PLANE + (pos[1] ^ (slot >> 4))).astype(F32)
+    chosen = (owner == sender) & (place == (slot & (SLOT - 1)))
+    return dot(chosen.astype(F32).astype(BF16), held)
 
 
 def add_into(out, base, terms, received):
@@ -337,25 +365,22 @@
         out[:, width:] = right.astype(out.dtype)
 
 
-def fill(base, entry, pieces, out_a, out_b):
-    terms = placed(out_a.shape[0], pieces)
+def fill(pos, base, owners, entry, pieces, out_a, out_b):
+    terms = placed(out_a.shape[0], pieces, owners[entry], pos)
     cut = out_a.shape[1]
     add_into(out_a, base[0][entry], terms[:, :cut], [])
     add_into(out_b, base[1][entry], terms[:, cut:], [])
 
 
-def first_kernel(base_a, base_b, d0, d1, d2, d3, out_a, out_b):
-    fill((base_a, base_b), 0, [d[...] for d in (d0, d1, d2, d3)], out_a, out_b)
-
-
-def next_kernel(base_a, base_b, d0, d1, d2, d3, out_a, out_b):
-    fill((base_a, base_b), 1, [d[...] for d in (d0, d1, d2, d3)], out_a, out_b)
-
-
-def rest_kernel(base_a, base_b, d0, d1, d2, d3, third_a, third_b, own_a, own_b):
+def fill_kernel(entry, pos, base_a, base_b, owners, d0, d1, d2, d3, out_a, out_b):
     pieces = [d[...] for d in (d0, d1, d2, d3)]
-    fill((base_a, base_b), 2, [d[0:SLOT] for d in pieces], third_a, third_b)
-    fill((base_a, base_b), 3, [d[SLOT:] for d in pieces], own_a, own_b)
+    fill(pos, (base_a, base_b), owners, entry, pieces, out_a, out_b)
+
+
+def rest_kernel(pos, base_a, base_b, owners, d0, d1, d2, d3, third_a, third_b, own_a, own_b):
+    pieces = [d[...] for d in (d0, d1, d2, d3)]
+    fill(pos, (base_a, base_b), owners, 2, [d[0:SLOT] for d in pieces], third_a, third_b)
+    fill(pos, (base_a, base_b), owners, 3, [d[SLOT:] for d in pieces], own_a, own_b)
 
 
 def second_kernel(pos, table, first, next_, received, out):
@@ -478,6 +503,8 @@
     requests_here = height // REQ_LEN
     capacity = 2 * requests_here
     half = width // 2
+    main = half * REQ_LEN // SLOT
+    sliced = -(-height // 8) * 8
     query_cols, key_cols = w_query.shape[1], w_keyvalue.shape[2]
     delta_cols = query_cols + key_cols
     cols = query_cols + 2 * key_cols
@@ -497,11 +524,11 @@
     in_hbm = pl.BlockSpec(memory_space=pltpu.HBM)
     slots = pl.pallas_call(
         functools.partial(dispatch_kernel, requests_here),
-        out_shape=shape((homes, SLOT, half), BF16),
+        out_shape=shape((homes, SLOT, main), BF16),
         in_specs=[SMEM, VMEM],
         out_specs=in_hbm,
         scratch_shapes=[
-            pltpu.VMEM((homes, SLOT, half), BF16),
+            pltpu.VMEM((homes, SLOT, main), BF16),
             pltpu.SemaphoreType.DMA((homes,)),
         ],
         compiler_params=PARAMS,
@@ -515,12 +542,11 @@
     down = adapter_down[0].reshape(width, 2 * local_rank)
 
     packed_rows = capacity * REQ_LEN
-    packed, select, marks = call(
+    packed, select = call(
         compact_kernel,
         [
             shape((packed_rows, half), BF16),
             shape((packed_rows, homes * SLOT), BF16),
-            shape((homes * SLOT, 128), BF16),
         ],
         [(pos, SMEM), (order, SMEM), (arrived, VMEM)],
         name="compact",
@@ -532,8 +558,8 @@
     packed_other = lax.ppermute(packed, "narrow", by_y)
     tokens, _ = barrier((tokens, packed))
     slices = call(
-        slices_kernel,
-        [shape((height, width // nz), BF16)] * nz,
+        functools.partial(slices_kernel, requests_here),
+        [shape((sliced, width // nz), BF16)] * nz,
         [(pos, SMEM), (tokens, VMEM)],
         name="slices",
     )
@@ -567,7 +593,6 @@
             (shrunk, VMEM),
             (shrunk_other, VMEM),
             (select, VMEM),
-            (marks, VMEM),
             (adapter_up_query[0], VMEM),
             (adapter_up_value[0], VMEM),
         ],
@@ -584,30 +609,34 @@
     slices = slices + [s3]
     kv_xc = plane(kv_x, by_c)
     padded = -(-height // SLOT) * SLOT
-    base_a, base_b = call(
+    base_a, base_b, owners = call(
         partial_kernel,
-        [shape((nz, height, chunk_cols), F32)] * 2,
+        [shape((nz, height, chunk_cols), F32)] * 2 + [shape((nz, 8, 128), BF16)],
         [(pos, SMEM), (inverse, SMEM)]
         + [(s, VMEM) for s in slices]
         + [(w, VMEM) for w in (w_query, q_c, q_x, q_xc, w_kv, kv_c, kv_x, kv_xc)],
         flops=2 * nz * height * width // nz * cols,
         nbytes=16 * 2**20,
-        scratch=[pltpu.VMEM((nz * (-(-height // 8) * 8), width // nz), BF16)],
+        scratch=[pltpu.VMEM((nz * sliced, width // nz), BF16)],
         name="partial",
     )
     block = shape((height, chunk_cols), BF16)
     wide_block = shape((height, chunk_cols), F32)
-    bases = [(base_a, VMEM), (base_b, VMEM)]
+    bases = [(pos, SMEM), (base_a, VMEM), (base_b, VMEM), (owners, VMEM)]
 
     def of(four):
         return [(p, VMEM) for p in four]
 
-    sent = call(first_kernel, [block, block], bases + of(first), name="reduce_first")
+    sent = call(
+        functools.partial(fill_kernel, 0), [block, block], bases + of(first), name="reduce_first"
+    )
     received = [lax.ppermute(s, "z", INWARD) for s in sent]
     pieces, _ = barrier((pieces, sent))
     next_ = over_plane(pieces[PLANE : 2 * PLANE])
     rest = over_plane(pieces[2 * PLANE :])
-    second = call(next_kernel, [wide_block] * 2, bases + of(next_), name="reduce_next")
+    second = call(
+        functools.partial(fill_kernel, 1), [wide_block] * 2, bases + of(next_), name="reduce_next"
+    )
     received[0], rest = barrier((received[0], rest))
     *third, own_a, own_b = call(rest_kernel, [wide_block] * 4, bases + of(rest), name="reduce_rest")
     scalars = [(pos, SMEM), (table, SMEM)]

time: 114 us -> 113 us (level)
  waiting for transfers between devices: 41.3 us -> 39.4 us
  starting transfers between devices: 49.4 us -> 47.7 us
  Pallas kernels: 17.5 us -> 19.1 us
    all_to_all x1, waiting for transfers between devices: 21 us -> 18.9 us  [reduce_body(): arrived = lax.all_to_all(slots, ('z', 'plane'), 0, 0, tiled=True)]
    pallas_call x15, Pallas kernels: 15.7 us -> 17.2 us  [call(): pl.pallas_call(kernel, out_shape=out_shape, in_specs=specs, out_specs=[VM...]
    ppermute x15, waiting for transfers between devices: 4.77 us -> 6.13 us  [plane(): return lax.ppermute(a, 'plane', perm)]
  transfers between devices with their start and end apart: 31 -> 31, of which waited for: 10 -> 12; matrix products, arithmetic and copies ran while one was open for 3% -> 3% of each run, Pallas kernels for 12% -> 13%
where the time goes in v2:
time: 113 us; the launch traced here: 111 us
  starting transfers between devices  47.7 us (42%)
  waiting for transfers between devices  39.4 us (35%)
  Pallas kernels  19.1 us (17%)
  local copies, waits for them, and re-layouts  4.92 us (4%)
    all_to_all x1, waiting for transfers between devices, reduce_body(): arrived = lax.all_to_all(slots, ('z', 'plane'), 0, 0, tiled=True)  18.9 us
    pallas_call x15, Pallas kernels, call(): pl.pallas_call(kernel, out_shape=out_shape, in_specs=specs, out_specs=[VM...  17.2 us
    ppermute x15, starting transfers between devices, plane(): return lax.ppermute(a, 'plane', perm)  11.5 us
    ppermute x3, starting transfers between devices, rotate_z(): return lax.ppermute(a, 'z', [(i, (i + shift) % nz) for i in range(nz)])  7.56 us
    all_to_all x1, starting transfers between devices, reduce_body(): arrived = lax.all_to_all(slots, ('z', 'plane'), 0, 0, tiled=True)  7.37 us
    ppermute x2, starting transfers between devices, reduce_body(): ends[chunk] = lax.ppermute(outer, 'z', PAIRS)  6.53 us
    ppermute x15, waiting for transfers between devices, plane(): return lax.ppermute(a, 'plane', perm)  6.13 us
    ppermute x2, waiting for transfers between devices, reduce_body(): ends[chunk] = lax.ppermute(outer, 'z', PAIRS)  5.61 us
  transfers between devices with their start and end apart: 31, of which 12 were waited for; matrix products, arithmetic and copies ran while one was open for 3% of the time, Pallas kernels for 13%

profile of v2, /device:TPU:0, one launch (start us, length us, event | category | flops | bytes accessed | tf_op | source)
XLA Modules:
  0.0 111.4 jit_solution(11282730580741558326)
XLA Ops:
  0.0 0.8 concatenate.3.pos
  0.8 1.1 copy-done
  1.9 1.8 %dispatch.1 = bf16[16,16,1792]{2,1,0:T(8,128)(2,1)} custom-call(s32[25]{0:T(128)S(1)} %concatenate.3.pos, bf16[84,4096]{1,0:T(8,128)(2,1)S(1)} %copy-done), custom_call_target="tpu_custom_call" | custom-call | tf_op jit(solution)/shard_map/dispatch/pallas_call | solution.py:525
  3.7 7.4 %all-to-all-start = ((bf16[16,16,1792]{2,1,0:T(8,128)(2,1)}), bf16[16,16,1792]{2,1,0:T(8,128)(2,1)S(1)}, u32[]{:S(2)}, u32[]{:S(2)}) async-start(bf16[16,16,1792]{2,1,0:T(8,128)(2,1)} %dispatch.1), calls=%async_computation | async-start | bytes 1835008 | tf_op jit(solution)/shard_map/all_to_all | solution.py:537
  11.1 2.0 %collective-permute-start.3 = (bf16[256,2048]{1,0:T(8,128)(2,1)S(1)}, bf16[256,2048]{1,0:T(8,128)(2,1)}, u32[]{:S(2)}, u32[]{:S(2)}) collective-permute-start(bf16[256,2048]{1,0:T(8,128)(2,1)S(1)} %copy-done.9), channel_id=1, source_target_pairs={{0,4},{4,0},{2,6},{6,2},{1,5},{5,1},{3,7},{7,3},{8,12},{12,8},{10,... | collective-permute-start | bytes 3145736 | tf_op jit(solution)/shard_map/ppermute | solution.py:521
  13.1 18.9 %all-to-all-done.arrived = bf16[16,16,1792]{2,1,0:T(8,128)(2,1)S(1)} async-done(((bf16[16,16,1792]{2,1,0:T(8,128)(2,1)}), bf16[16,16,1792]{2,1,0:T(8,128)(2,1)S(1)}, u32[]{:S(2)}, u32[]{:S(2)}) %all-to-all-start) | async-done | bytes 917536 | tf_op jit(solution)/shard_map/all_to_all | solution.py:537
  32.0 1.6 %compact.1 = (bf16[168,2048]{1,0:T(8,128)(2,1)S(1)}, bf16[168,256]{1,0:T(8,128)(2,1)S(1)}) custom-call(s32[25]{0:T(128)S(1)} %concatenate.3.pos, s32[4,4]{1,0:T(4,128)S(1)} %copy-done.6, bf16[16,16,1792]{2,1,0:T(8,128)(2,1)S(1)} %all-to-all-done.arrived), custom_call_target="tpu_custom_call" | custom-call | tf_op jit(solution)/shard_map/compact/pallas_call | solution.py:167
  33.5 1.6 %collective-permute-start = (bf16[168,2048]{1,0:T(8,128)(2,1)S(1)}, bf16[168,2048]{1,0:T(8,128)(2,1)S(1)}, u32[]{:S(2)}, u32[]{:S(2)}) collective-permute-start(bf16[168,2048]{1,0:T(8,128)(2,1)S(1)} %get-tuple-element.75.own), channel_id=1, source_target_pairs={{0,1},{1,0},{2,3},{3,2},{4,5},{5,4},{6,7},{7,6},{8,9},{9,8},{10,11... | collective-permute-start | bytes 2064392 | tf_op jit(solution)/shard_map/ppermute | solution.py:558
  35.2 0.6 slices.1
  35.8 2.8 %collective-permute-start.1 = (bf16[88,1024]{1,0:T(8,128)(2,1)S(1)}, bf16[88,1024]{1,0:T(8,128)(2,1)S(1)}, u32[]{:S(2)}, u32[]{:S(2)}) collective-permute-start(bf16[88,1024]{1,0:T(8,128)(2,1)S(1)} %get-tuple-element.78), channel_id=1, source_target_pairs={{0,8},{8,16},{16,24},{24,0},{1,9},{9,17},{17,25},{25,1},{2,10},{10... | collective-permute-start | bytes 540680 | tf_op jit(solution)/shard_map/ppermute | solution.py:556
  38.6 1.8 %collective-permute-start.2 = (bf16[88,1024]{1,0:T(8,128)(2,1)S(1)}, bf16[88,1024]{1,0:T(8,128)(2,1)S(1)}, u32[]{:S(2)}, u32[]{:S(2)}) collective-permute-start(bf16[88,1024]{1,0:T(8,128)(2,1)S(1)} %get-tuple-element.79), channel_id=1, source_target_pairs={{0,16},{8,24},{16,0},{24,8},{1,17},{9,25},{17,1},{25,9},{2,18},{10... | collective-permute-start | bytes 540680 | tf_op jit(solution)/shard_map/ppermute | solution.py:556
  40.4 0.1 copy.15
  40.4 1.5 %collective-permute-start.5 = (bf16[256,1024]{1,0:T(8,128)(2,1)S(1)}, bf16[256,1024]{1,0:T(8,128)(2,1)S(1)}, u32[]{:S(2)}, u32[]{:S(2)}) collective-permute-start(bf16[256,1024]{1,0:T(8,128)(2,1)S(1)} %bitcast.14), channel_id=1, source_target_pairs={{0,4},{4,0},{2,6},{6,2},{1,5},{5,1},{3,7},{7,3},{8,12},{12,8},{10,... | collective-permute-start | bytes 1572872 | tf_op jit(solution)/shard_map/ppermute | solution.py:521
  41.9 2.9 %copy.16 = bf16[512,8,2,256]{3,1,2,0:T(8,128)(2,1)S(1)} copy(bf16[512,8,2,256]{3,2,1,0:T(2,128)(2,1)} %bitcast.17) | data formatting | bytes 8388608
  44.9 1.1 shrink.1.total
  46.0 1.1 %collective-permute-done.3.q2 = bf16[256,2048]{1,0:T(8,128)(2,1)} collective-permute-done((bf16[256,2048]{1,0:T(8,128)(2,1)S(1)}, bf16[256,2048]{1,0:T(8,128)(2,1)}, u32[]{:S(2)}, u32[]{:S(2)}) %collective-permute-start.3) | collective-permute-done | bytes 1048608 | tf_op jit(solution)/shard_map/ppermute | solution.py:521
  47.1 4.8 %collective-permute-done.2.s2 = bf16[88,1024]{1,0:T(8,128)(2,1)S(1)} collective-permute-done((bf16[88,1024]{1,0:T(8,128)(2,1)S(1)}, bf16[88,1024]{1,0:T(8,128)(2,1)S(1)}, u32[]{:S(2)}, u32[]{:S(2)}) %collective-permute-start.2) | collective-permute-done | bytes 180256 | tf_op jit(solution)/shard_map/ppermute | solution.py:556
  51.9 1.1 shrink_rest.1.own
  53.0 0.0 copy-start.10
  53.0 0.1 collective-permute-start.7
  53.1 0.5 collective-permute-start.8
  53.6 0.9 collective-permute-start.4
  54.5 3.0 %collective-permute-start.6 = (bf16[88,1024]{1,0:T(8,128)(2,1)S(1)}, bf16[88,1024]{1,0:T(8,128)(2,1)S(1)}, u32[]{:S(2)}, u32[]{:S(2)}) collective-permute-start(bf16[88,1024]{1,0:T(8,128)(2,1)S(1)} %get-tuple-element.89), channel_id=1, source_target_pairs={{0,24},{8,0},{16,8},{24,16},{1,25},{9,1},{17,9},{25,17},{2,26},{10... | collective-permute-start | bytes 540680 | tf_op jit(solution)/shard_map/ppermute | solution.py:556
  57.5 0.2 collective-permute-done.5.v2
  57.8 2.5 %collective-permute-done.4.other = bf16[184,512]{1,0:T(8,128)(2,1)S(1)} collective-permute-done((bf16[184,512]{1,0:T(8,128)(2,1)S(1)}, bf16[184,512]{1,0:T(8,128)(2,1)S(1)}, u32[]{:S(2)}, u32[]{:S(2)}) %collective-permute-start.4) | collective-permute-done | bytes 188448 | tf_op jit(solution)/shard_map/ppermute | solution.py:581
  60.3 1.6 %expand.1 = (bf16[16,2560]{1,0:T(8,128)(2,1)S(1)}, bf16[16,2560]{1,0:T(8,128)(2,1)S(1)}, bf16[16,2560]{1,0:T(8,128)(2,1)S(1)}, bf16[16,2560]{1,0:T(8,128)(2,1)S(...) custom-call(s32[25]{0:T(128)S(1)} %concatenate.3.pos, ...), custom_call_target="tpu_custom_call" | custom-call | tf_op jit(solution)/shard_map/expand/pallas_call | solution.py:167
  61.9 0.1 collective-permute-done.6.s3
  62.1 0.5 collective-permute-start.11
  62.6 1.7 %collective-permute-start.12 = (bf16[16,2560]{1,0:T(8,128)(2,1)S(1)}, bf16[16,2560]{1,0:T(8,128)(2,1)S(1)}, u32[]{:S(2)}, u32[]{:S(2)}) collective-permute-start(bf16[16,2560]{1,0:T(8,128)(2,1)S(1)} %get-tuple-element.94), channel_id=1, source_target_pairs={{0,4},{4,0},{2,6},{6,2},{1,5},{5,1},{3,7},{7,3},{8,12},{12,8},{10,... | collective-permute-start | bytes 245768 | tf_op jit(solution)/shard_map/ppermute | solution.py:521
  64.3 1.1 %collective-permute-start.13 = (bf16[16,2560]{1,0:T(8,128)(2,1)S(1)}, bf16[16,2560]{1,0:T(8,128)(2,1)S(1)}, u32[]{:S(2)}, u32[]{:S(2)}) collective-permute-start(bf16[16,2560]{1,0:T(8,128)(2,1)S(1)} %get-tuple-element.95), channel_id=1, source_target_pairs={{0,6},{6,0},{2,4},{4,2},{1,7},{7,1},{3,5},{5,3},{8,14},{14,8},{10,... | collective-permute-start | bytes 245768 | tf_op jit(solution)/shard_map/ppermute | solution.py:521
  65.5 3.7 %partial.1 = (f32[4,84,1536]{2,1,0:T(8,128)S(1)}, f32[4,84,1536]{2,1,0:T(8,128)S(1)}, bf16[4,8,128]{2,1,0:T(8,128)(2,1)S(1)}) custom-call(s32[25]{0:T(128)S(1)} %concatenate.3.pos, s32[4,4]{1,0:T(4,128)S(1)} %copy-done.10, bf16[88,1024]{1,0:T(8,128)(2,1)S(1)} %get-tuple-element.104.s0, bf16[88,1024]{1,0:T(8,128)(2,1)S(1)} %collective-permute-done.1.s1, ...), custom_call_target="tpu_custom_call" | custom-call | flops 2113929216 | bytes 16777216 | tf_op jit(solution)/shard_map/partial/pallas_call | solution.py:167
  69.2 1.0 reduce_first.1
  70.2 4.3 %collective-permute-start.25 = (bf16[84,1536]{1,0:T(8,128)(2,1)S(1)}, bf16[84,1536]{1,0:T(8,128)(2,1)S(1)}, u32[]{:S(2)}, u32[]{:S(2)}) collective-permute-start(bf16[84,1536]{1,0:T(8,128)(2,1)S(1)} %get-tuple-element.116.first), channel_id=1, source_target_pairs={{0,8},{24,16},{1,9},{25,17},{2,10},{26,18},{3,11},{27,19},{4,12},{... | collective-permute-start | bytes 774152 | tf_op jit(solution)/shard_map/ppermute | solution.py:633
  74.5 0.0 copy-start.7
  74.5 1.3 %collective-permute-start.14 = (bf16[84,1536]{1,0:T(8,128)(2,1)S(1)}, bf16[84,1536]{1,0:T(8,128)(2,1)S(1)}, u32[]{:S(2)}, u32[]{:S(2)}) collective-permute-start(bf16[84,1536]{1,0:T(8,128)(2,1)S(1)} %get-tuple-element.115.first), channel_id=1, source_target_pairs={{0,8},{24,16},{1,9},{25,17},{2,10},{26,18},{3,11},{27,19},{4,12},{... | collective-permute-start | bytes 774152 | tf_op jit(solution)/shard_map/ppermute | solution.py:633
  75.8 0.1 collective-permute-start.18
  75.9 1.1 collective-permute-start.19
  77.0 0.7 collective-permute-start.20
  77.8 0.3 collective-permute-start.15
  78.1 3.1 %collective-permute-done.19.d2 = bf16[16,2560]{1,0:T(8,128)(2,1)S(1)} collective-permute-done((bf16[16,2560]{1,0:T(8,128)(2,1)S(1)}, bf16[16,2560]{1,0:T(8,128)(2,1)S(1)}, u32[]{:S(2)}, u32[]{:S(2)}) %collective-permute-start.19) | collective-permute-done | bytes 81952 | tf_op jit(solution)/shard_map/ppermute | solution.py:521
  81.2 1.1 collective-permute-start.16
  82.3 0.7 collective-permute-start.17
  83.0 1.0 reduce_next.1
  84.0 0.6 reduce_second.3
  84.6 1.7 %collective-permute-start.26 = (bf16[84,1536]{1,0:T(8,128)(2,1)S(1)}, bf16[84,1536]{1,0:T(8,128)(2,1)S(1)}, u32[]{:S(2)}, u32[]{:S(2)}) collective-permute-start(bf16[84,1536]{1,0:T(8,128)(2,1)S(1)} %reduce_second.3), channel_id=1, source_target_pairs={{0,8},{24,16},{1,9},{25,17},{2,10},{26,18},{3,11},{27,19},{4,12},{... | collective-permute-start | bytes 774152 | tf_op jit(solution)/shard_map/ppermute | solution.py:652
  86.3 0.7 collective-permute-start.27
  87.0 0.9 collective-permute-done.16.d2
  87.9 0.8 collective-permute-done.17.d3
  88.7 0.6 reduce_second.2
  89.3 2.2 %collective-permute-start.21 = (bf16[84,1536]{1,0:T(8,128)(2,1)S(1)}, bf16[84,1536]{1,0:T(8,128)(2,1)S(1)}, u32[]{:S(2)}, u32[]{:S(2)}) collective-permute-start(bf16[84,1536]{1,0:T(8,128)(2,1)S(1)} %reduce_second.2), channel_id=1, source_target_pairs={{0,8},{24,16},{1,9},{25,17},{2,10},{26,18},{3,11},{27,19},{4,12},{... | collective-permute-start | bytes 774152 | tf_op jit(solution)/shard_map/ppermute | solution.py:652
  91.5 0.7 collective-permute-start.22
  92.2 1.3 %reduce_rest.1 = (f32[84,1536]{1,0:T(8,128)S(1)}, f32[84,1536]{1,0:T(8,128)S(1)}, f32[84,1536]{1,0:T(8,128)S(1)}, f32[84,1536]{1,0:T(8,128)S(1)}) custom-call(s32[25]{0:T(128)S(1)} %concatenate.3.pos, f32[4,84,1536]{2,1,0:T(8,128)S(1)} %get-tuple-element.112.base_a, f32[4,84,1536]{2,1,0:T(8,128)S(1)} %get-tuple-element.113.base_b, ...), custom_call_target="tpu_custom_call" | custom-call | tf_op jit(solution)/shard_map/reduce_rest/pallas_call | solution.py:167
  93.6 0.0 copy-start.5
  93.6 0.1 reduce_third.3
  93.7 2.8 %collective-permute-start.28 = (bf16[84,1536]{1,0:T(8,128)(2,1)S(1)}, bf16[84,1536]{1,0:T(8,128)(2,1)S(1)}, u32[]{:S(2)}, u32[]{:S(2)}) collective-permute-start(bf16[84,1536]{1,0:T(8,128)(2,1)S(1)} %get-tuple-element.138), channel_id=1, source_target_pairs={{0,8},{8,0},{16,24},{24,16},{1,9},{9,1},{17,25},{25,17},{2,10},{10... | collective-permute-start | bytes 774152 | tf_op jit(solution)/shard_map/ppermute | solution.py:661
  96.5 0.7 collective-permute-start.29
  97.2 1.3 %collective-permute-done.21.from_end = bf16[84,1536]{1,0:T(8,128)(2,1)S(1)} collective-permute-done((bf16[84,1536]{1,0:T(8,128)(2,1)S(1)}, bf16[84,1536]{1,0:T(8,128)(2,1)S(1)}, u32[]{:S(2)}, u32[]{:S(2)}) %collective-permute-start.21) | collective-permute-done | bytes 258080 | tf_op jit(solution)/shard_map/ppermute | solution.py:652
  98.5 0.1 reduce_third.2
  98.6 3.7 %collective-permute-start.23 = (bf16[84,1536]{1,0:T(8,128)(2,1)S(1)}, bf16[84,1536]{1,0:T(8,128)(2,1)S(1)}, u32[]{:S(2)}, u32[]{:S(2)}) collective-permute-start(bf16[84,1536]{1,0:T(8,128)(2,1)S(1)} %get-tuple-element.133), channel_id=1, source_target_pairs={{0,8},{8,0},{16,24},{24,16},{1,9},{9,1},{17,25},{25,17},{2,10},{10... | collective-permute-start | bytes 774152 | tf_op jit(solution)/shard_map/ppermute | solution.py:661
  102.3 0.7 collective-permute-start.24
  103.0 1.3 %collective-permute-done.28.up = bf16[84,1536]{1,0:T(8,128)(2,1)S(1)} collective-permute-done((bf16[84,1536]{1,0:T(8,128)(2,1)S(1)}, bf16[84,1536]{1,0:T(8,128)(2,1)S(1)}, u32[]{:S(2)}, u32[]{:S(2)}) %collective-permute-start.28) | collective-permute-done | bytes 258080 | tf_op jit(solution)/shard_map/ppermute | solution.py:661
  104.3 1.2 %attend_near.1 = (bf16[84,512]{1,0:T(8,128)(2,1)S(1)}, bf16[4,128,128]{2,1,0:T(8,128)(2,1)S(1)}, bf16[4,128,128]{2,1,0:T(8,128)(2,1)S(1)}, f32[384,128]{1,0:T(8,128)S(1)}, f32[384,128]{1,0:T(8,128)S(1)}) custom-call(s32[6]{0:T(128)S(1)} %copy-done.8, f32[84,1536]{1,0:T(8,128)S(1)} %get-tuple-element.135.own, ...), custom_call_target="tpu_custom_call" | custom-call | bytes 8388608 | tf_op jit(solution)/shard_map/attend_near/pallas_call | solution.py:167
  105.5 4.3 %collective-permute-done.23.up = bf16[84,1536]{1,0:T(8,128)(2,1)S(1)} collective-permute-done((bf16[84,1536]{1,0:T(8,128)(2,1)S(1)}, bf16[84,1536]{1,0:T(8,128)(2,1)S(1)}, u32[]{:S(2)}, u32[]{:S(2)}) %collective-permute-start.23) | collective-permute-done | bytes 258080 | tf_op jit(solution)/shard_map/ppermute | solution.py:661
  109.8 1.6 %attend.1 = bf16[84,2048]{1,0:T(8,128)(2,1)} custom-call(f32[84,1536]{1,0:T(8,128)S(1)} %get-tuple-element.125.own, bf16[84,1536]{1,0:T(8,128)(2,1)S(1)} %collective-permute-done.23.up, bf16[84,1536]{1,0:T(8,128)(2,1)S(1)} %collective-permute-done.24.down, bf16[84,512]{1,0:T(8,128)(2,1)S(1)} %get-tuple-element.140.near, ...), custom_call_target="tpu_custom_call" | custom-call | tf_op jit(solution)/shard_map/attend/pallas_call | solution.py:167
  (41 shorter events, 0.1 us)
Async XLA Ops:
  0.0 32.0 %copy-start.6 = (s32[4,4]{1,0:T(4,128)S(1)}, s32[4,4]{1,0:T(4,128)}, u32[]{:S(2)}) copy-start(s32[4,4]{1,0:T(4,128)} %constant.21.clone.order) | copy-start | bytes 196
  0.8 1.1 %copy-start = (bf16[84,4096]{1,0:T(8,128)(2,1)S(1)}, bf16[84,4096]{1,0:T(8,128)(2,1)}, u32[]{:S(2)}) copy-start(bf16[84,4096]{1,0:T(8,128)(2,1)} %tokens.2) | copy-start | bytes 2064388
  1.9 9.2 %copy-start.9 = (bf16[256,2048]{1,0:T(8,128)(2,1)S(1)}, bf16[256,2048]{1,0:T(8,128)(2,1)}, u32[]{:S(2)}) copy-start(bf16[256,2048]{1,0:T(8,128)(2,1)} %q0) | copy-start | bytes 3145732
  1.9 33.3 %copy-start.1 = (bf16[84,4096]{1,0:T(8,128)(2,1)S(1)}, bf16[84,4096]{1,0:T(8,128)(2,1)}, u32[]{:S(2)}) copy-start(bf16[84,4096]{1,0:T(8,128)(2,1)} %tokens.2) | copy-start | bytes 2064388
  1.9 38.5 %copy-start.11 = (bf16[256,2,512]{2,1,0:T(2,128)(2,1)S(1)}, bf16[256,2,512]{2,1,0:T(2,128)(2,1)}, u32[]{:S(2)}) copy-start(bf16[256,2,512]{2,1,0:T(2,128)(2,1)} %param.16) | copy-start | bytes 1572868
  3.7 28.2 %all-to-all-start = ((bf16[16,16,1792]{2,1,0:T(8,128)(2,1)}), bf16[16,16,1792]{2,1,0:T(8,128)(2,1)S(1)}, u32[]{:S(2)}, u32[]{:S(2)}) async-start(bf16[16,16,1792]{2,1,0:T(8,128)(2,1)} %dispatch.1), calls=%async_computation | async-start | bytes 1835008 | tf_op jit(solution)/shard_map/all_to_all | solution.py:537
  11.1 36.0 %collective-permute-start.3 = (bf16[256,2048]{1,0:T(8,128)(2,1)S(1)}, bf16[256,2048]{1,0:T(8,128)(2,1)}, u32[]{:S(2)}, u32[]{:S(2)}) collective-permute-start(bf16[256,2048]{1,0:T(8,128)(2,1)S(1)} %copy-done.9), channel_id=1, source_target_pairs={{0,4},{4,0},{2,6},{6,2},{1,5},{5,1},{3,7},{7,3},{8,12},{12,8},{10,... | collective-permute-start | bytes 3145736 | tf_op jit(solution)/shard_map/ppermute | solution.py:521
  33.5 18.4 %collective-permute-start = (bf16[168,2048]{1,0:T(8,128)(2,1)S(1)}, bf16[168,2048]{1,0:T(8,128)(2,1)S(1)}, u32[]{:S(2)}, u32[]{:S(2)}) collective-permute-start(bf16[168,2048]{1,0:T(8,128)(2,1)S(1)} %get-tuple-element.75.own), channel_id=1, source_target_pairs={{0,1},{1,0},{2,3},{3,2},{4,5},{5,4},{6,7},{7,6},{8,9},{9,8},{10,11... | collective-permute-start | bytes 2064392 | tf_op jit(solution)/shard_map/ppermute | solution.py:558
  35.8 11.3 %collective-permute-start.1 = (bf16[88,1024]{1,0:T(8,128)(2,1)S(1)}, bf16[88,1024]{1,0:T(8,128)(2,1)S(1)}, u32[]{:S(2)}, u32[]{:S(2)}) collective-permute-start(bf16[88,1024]{1,0:T(8,128)(2,1)S(1)} %get-tuple-element.78), channel_id=1, source_target_pairs={{0,8},{8,16},{16,24},{24,0},{1,9},{9,17},{17,25},{25,1},{2,10},{10... | collective-permute-start | bytes 540680 | tf_op jit(solution)/shard_map/ppermute | solution.py:556
  38.6 13.3 %collective-permute-start.2 = (bf16[88,1024]{1,0:T(8,128)(2,1)S(1)}, bf16[88,1024]{1,0:T(8,128)(2,1)S(1)}, u32[]{:S(2)}, u32[]{:S(2)}) collective-permute-start(bf16[88,1024]{1,0:T(8,128)(2,1)S(1)} %get-tuple-element.79), channel_id=1, source_target_pairs={{0,16},{8,24},{16,0},{24,8},{1,17},{9,25},{17,1},{25,9},{2,18},{10... | collective-permute-start | bytes 540680 | tf_op jit(solution)/shard_map/ppermute | solution.py:556
  40.4 17.3 %collective-permute-start.5 = (bf16[256,1024]{1,0:T(8,128)(2,1)S(1)}, bf16[256,1024]{1,0:T(8,128)(2,1)S(1)}, u32[]{:S(2)}, u32[]{:S(2)}) collective-permute-start(bf16[256,1024]{1,0:T(8,128)(2,1)S(1)} %bitcast.14), channel_id=1, source_target_pairs={{0,4},{4,0},{2,6},{6,2},{1,5},{5,1},{3,7},{7,3},{8,12},{12,8},{10,... | collective-permute-start | bytes 1572872 | tf_op jit(solution)/shard_map/ppermute | solution.py:521
  46.0 14.3 %copy-start.2 = (bf16[1,512,2048]{2,1,0:T(8,128)(2,1)S(1)}, bf16[1,512,2048]{2,1,0:T(8,128)(2,1)}, u32[]{:S(2)}) copy-start(bf16[1,512,2048]{2,1,0:T(8,128)(2,1)} %param.18) | copy-start | bytes 6291460
  46.0 14.3 %copy-start.3 = (bf16[1,512,512]{2,1,0:T(8,128)(2,1)S(1)}, bf16[1,512,512]{2,1,0:T(8,128)(2,1)}, u32[]{:S(2)}) copy-start(bf16[1,512,512]{2,1,0:T(8,128)(2,1)} %param.19) | copy-start | bytes 1572868
  53.0 12.5 %copy-start.10 = (s32[4,4]{1,0:T(4,128)S(1)}, s32[4,4]{1,0:T(4,128)}, u32[]{:S(2)}) copy-start(s32[4,4]{1,0:T(4,128)} %constant.22.clone.inverse) | copy-start | bytes 196
  53.0 12.4 %collective-permute-start.7 = (bf16[256,2048]{1,0:T(8,128)(2,1)S(1)}, bf16[256,2048]{1,0:T(8,128)(2,1)S(1)}, u32[]{:S(2)}, u32[]{:S(2)}) collective-permute-start(bf16[256,2048]{1,0:T(8,128)(2,1)S(1)} %copy-done.9), channel_id=1, source_target_pairs={{0,2},{2,0},{4,6},{6,4},{1,3},{3,1},{5,7},{7,5},{8,10},{10,8},{12,... | collective-permute-start | bytes 3145736 | tf_op jit(solution)/shard_map/ppermute | solution.py:521
  53.1 12.4 %collective-permute-start.8 = (bf16[256,2048]{1,0:T(8,128)(2,1)}, bf16[256,2048]{1,0:T(8,128)(2,1)S(1)}, u32[]{:S(2)}, u32[]{:S(2)}) collective-permute-start(bf16[256,2048]{1,0:T(8,128)(2,1)} %collective-permute-done.3.q2), channel_id=1, source_target_pairs={{0,2},{2,0},{4,6},{6,4},{1,3},{3,1},{5,7},{7,5},{8,10},{10,8},{12,... | collective-permute-start | bytes 3145736 | tf_op jit(solution)/shard_map/ppermute | solution.py:521
  53.6 6.7 %collective-permute-start.4 = (bf16[184,512]{1,0:T(8,128)(2,1)S(1)}, bf16[184,512]{1,0:T(8,128)(2,1)S(1)}, u32[]{:S(2)}, u32[]{:S(2)}) collective-permute-start(bf16[184,512]{1,0:T(8,128)(2,1)S(1)} %shrink_rest.1.own), channel_id=1, source_target_pairs={{0,1},{1,0},{2,3},{3,2},{4,5},{5,4},{6,7},{7,6},{8,9},{9,8},{10,11... | collective-permute-start | bytes 565256 | tf_op jit(solution)/shard_map/ppermute | solution.py:581
  54.5 7.5 %collective-permute-start.6 = (bf16[88,1024]{1,0:T(8,128)(2,1)S(1)}, bf16[88,1024]{1,0:T(8,128)(2,1)S(1)}, u32[]{:S(2)}, u32[]{:S(2)}) collective-permute-start(bf16[88,1024]{1,0:T(8,128)(2,1)S(1)} %get-tuple-element.89), channel_id=1, source_target_pairs={{0,24},{8,0},{16,8},{24,16},{1,25},{9,1},{17,9},{25,17},{2,26},{10... | collective-permute-start | bytes 540680 | tf_op jit(solution)/shard_map/ppermute | solution.py:556
  57.8 4.8 %collective-permute-start.9 = (bf16[256,1024]{1,0:T(8,128)(2,1)S(1)}, bf16[256,1024]{1,0:T(8,128)(2,1)S(1)}, u32[]{:S(2)}, u32[]{:S(2)}) collective-permute-start(bf16[256,1024]{1,0:T(8,128)(2,1)S(1)} %bitcast.15), channel_id=1, source_target_pairs={{0,2},{2,0},{4,6},{6,4},{1,3},{3,1},{5,7},{7,5},{8,10},{10,8},{12,... | collective-permute-start | bytes 1572872 | tf_op jit(solution)/shard_map/ppermute | solution.py:521
  62.1 2.3 %collective-permute-start.10 = (bf16[256,1024]{1,0:T(8,128)(2,1)S(1)}, bf16[256,1024]{1,0:T(8,128)(2,1)S(1)}, u32[]{:S(2)}, u32[]{:S(2)}) collective-permute-start(bf16[256,1024]{1,0:T(8,128)(2,1)S(1)} %collective-permute-done.5.v2), channel_id=1, source_target_pairs={{0,2},{2,0},{4,6},{6,4},{1,3},{3,1},{5,7},{7,5},{8,10},{10,8},{12,... | collective-permute-start | bytes 1572872 | tf_op jit(solution)/shard_map/ppermute | solution.py:521
  62.1 7.1 %collective-permute-start.11 = (bf16[16,2560]{1,0:T(8,128)(2,1)S(1)}, bf16[16,2560]{1,0:T(8,128)(2,1)S(1)}, u32[]{:S(2)}, u32[]{:S(2)}) collective-permute-start(bf16[16,2560]{1,0:T(8,128)(2,1)S(1)} %get-tuple-element.93), channel_id=1, source_target_pairs={{0,2},{2,0},{4,6},{6,4},{1,3},{3,1},{5,7},{7,5},{8,10},{10,8},{12,... | collective-permute-start | bytes 245768 | tf_op jit(solution)/shard_map/ppermute | solution.py:521
  62.6 6.6 %collective-permute-start.12 = (bf16[16,2560]{1,0:T(8,128)(2,1)S(1)}, bf16[16,2560]{1,0:T(8,128)(2,1)S(1)}, u32[]{:S(2)}, u32[]{:S(2)}) collective-permute-start(bf16[16,2560]{1,0:T(8,128)(2,1)S(1)} %get-tuple-element.94), channel_id=1, source_target_pairs={{0,4},{4,0},{2,6},{6,2},{1,5},{5,1},{3,7},{7,3},{8,12},{12,8},{10,... | collective-permute-start | bytes 245768 | tf_op jit(solution)/shard_map/ppermute | solution.py:521
  64.3 4.8 %collective-permute-start.13 = (bf16[16,2560]{1,0:T(8,128)(2,1)S(1)}, bf16[16,2560]{1,0:T(8,128)(2,1)S(1)}, u32[]{:S(2)}, u32[]{:S(2)}) collective-permute-start(bf16[16,2560]{1,0:T(8,128)(2,1)S(1)} %get-tuple-element.95), channel_id=1, source_target_pairs={{0,6},{6,0},{2,4},{4,2},{1,7},{7,1},{3,5},{5,3},{8,14},{14,8},{10,... | collective-permute-start | bytes 245768 | tf_op jit(solution)/shard_map/ppermute | solution.py:521
  70.2 13.8 %collective-permute-start.25 = (bf16[84,1536]{1,0:T(8,128)(2,1)S(1)}, bf16[84,1536]{1,0:T(8,128)(2,1)S(1)}, u32[]{:S(2)}, u32[]{:S(2)}) collective-permute-start(bf16[84,1536]{1,0:T(8,128)(2,1)S(1)} %get-tuple-element.116.first), channel_id=1, source_target_pairs={{0,8},{24,16},{1,9},{25,17},{2,10},{26,18},{3,11},{27,19},{4,12},{... | collective-permute-start | bytes 774152 | tf_op jit(solution)/shard_map/ppermute | solution.py:633
  74.5 9.5 %copy-start.7 = (s32[1,4]{1,0:T(1,128)S(1)}, s32[1,4]{1,0:T(1,128)}, u32[]{:S(2)}) copy-start(s32[1,4]{1,0:T(1,128)} %constant.23.clone.table) | copy-start | bytes 52
  74.5 14.2 %collective-permute-start.14 = (bf16[84,1536]{1,0:T(8,128)(2,1)S(1)}, bf16[84,1536]{1,0:T(8,128)(2,1)S(1)}, u32[]{:S(2)}, u32[]{:S(2)}) collective-permute-start(bf16[84,1536]{1,0:T(8,128)(2,1)S(1)} %get-tuple-element.115.first), channel_id=1, source_target_pairs={{0,8},{24,16},{1,9},{25,17},{2,10},{26,18},{3,11},{27,19},{4,12},{... | collective-permute-start | bytes 774152 | tf_op jit(solution)/shard_map/ppermute | solution.py:633
  75.8 1.9 %collective-permute-start.18 = (bf16[16,2560]{1,0:T(8,128)(2,1)S(1)}, bf16[16,2560]{1,0:T(8,128)(2,1)S(1)}, u32[]{:S(2)}, u32[]{:S(2)}) collective-permute-start(bf16[16,2560]{1,0:T(8,128)(2,1)S(1)} %get-tuple-element.127), channel_id=1, source_target_pairs={{0,2},{2,0},{4,6},{6,4},{1,3},{3,1},{5,7},{7,5},{8,10},{10,8},{12,... | collective-permute-start | bytes 245768 | tf_op jit(solution)/shard_map/ppermute | solution.py:521
  75.9 5.3 %collective-permute-start.19 = (bf16[16,2560]{1,0:T(8,128)(2,1)S(1)}, bf16[16,2560]{1,0:T(8,128)(2,1)S(1)}, u32[]{:S(2)}, u32[]{:S(2)}) collective-permute-start(bf16[16,2560]{1,0:T(8,128)(2,1)S(1)} %get-tuple-element.128), channel_id=1, source_target_pairs={{0,4},{4,0},{2,6},{6,2},{1,5},{5,1},{3,7},{7,3},{8,12},{12,8},{10,... | collective-permute-start | bytes 245768 | tf_op jit(solution)/shard_map/ppermute | solution.py:521
  77.0 5.2 %collective-permute-start.20 = (bf16[16,2560]{1,0:T(8,128)(2,1)S(1)}, bf16[16,2560]{1,0:T(8,128)(2,1)S(1)}, u32[]{:S(2)}, u32[]{:S(2)}) collective-permute-start(bf16[16,2560]{1,0:T(8,128)(2,1)S(1)} %get-tuple-element.129), channel_id=1, source_target_pairs={{0,6},{6,0},{2,4},{4,2},{1,7},{7,1},{3,5},{5,3},{8,14},{14,8},{10,... | collective-permute-start | bytes 245768 | tf_op jit(solution)/shard_map/ppermute | solution.py:521
  77.8 8.6 %collective-permute-start.15 = (bf16[32,2560]{1,0:T(8,128)(2,1)S(1)}, bf16[32,2560]{1,0:T(8,128)(2,1)S(1)}, u32[]{:S(2)}, u32[]{:S(2)}) collective-permute-start(bf16[32,2560]{1,0:T(8,128)(2,1)S(1)} %get-tuple-element.118), channel_id=1, source_target_pairs={{0,2},{2,0},{4,6},{6,4},{1,3},{3,1},{5,7},{7,5},{8,10},{10,8},{12,... | collective-permute-start | bytes 491528 | tf_op jit(solution)/shard_map/ppermute | solution.py:521
  81.2 6.7 %collective-permute-start.16 = (bf16[32,2560]{1,0:T(8,128)(2,1)S(1)}, bf16[32,2560]{1,0:T(8,128)(2,1)S(1)}, u32[]{:S(2)}, u32[]{:S(2)}) collective-permute-start(bf16[32,2560]{1,0:T(8,128)(2,1)S(1)} %get-tuple-element.119), channel_id=1, source_target_pairs={{0,4},{4,0},{2,6},{6,2},{1,5},{5,1},{3,7},{7,3},{8,12},{12,8},{10,... | collective-permute-start | bytes 491528 | tf_op jit(solution)/shard_map/ppermute | solution.py:521
  82.3 6.4 %collective-permute-start.17 = (bf16[32,2560]{1,0:T(8,128)(2,1)S(1)}, bf16[32,2560]{1,0:T(8,128)(2,1)S(1)}, u32[]{:S(2)}, u32[]{:S(2)}) collective-permute-start(bf16[32,2560]{1,0:T(8,128)(2,1)S(1)} %get-tuple-element.120), channel_id=1, source_target_pairs={{0,6},{6,0},{2,4},{4,2},{1,7},{7,1},{3,5},{5,3},{8,14},{14,8},{10,... | collective-permute-start | bytes 491528 | tf_op jit(solution)/shard_map/ppermute | solution.py:521
  84.6 9.0 %collective-permute-start.26 = (bf16[84,1536]{1,0:T(8,128)(2,1)S(1)}, bf16[84,1536]{1,0:T(8,128)(2,1)S(1)}, u32[]{:S(2)}, u32[]{:S(2)}) collective-permute-start(bf16[84,1536]{1,0:T(8,128)(2,1)S(1)} %reduce_second.3), channel_id=1, source_target_pairs={{0,8},{24,16},{1,9},{25,17},{2,10},{26,18},{3,11},{27,19},{4,12},{... | collective-permute-start | bytes 774152 | tf_op jit(solution)/shard_map/ppermute | solution.py:652
  86.3 7.3 %collective-permute-start.27 = (bf16[84,1536]{1,0:T(8,128)(2,1)S(1)}, bf16[84,1536]{1,0:T(8,128)(2,1)S(1)}, u32[]{:S(2)}, u32[]{:S(2)}) collective-permute-start(bf16[84,1536]{1,0:T(8,128)(2,1)S(1)} %reduce_second.3), channel_id=1, source_target_pairs={{8,16},{16,8},{9,17},{17,9},{10,18},{18,10},{11,19},{19,11},{12,20... | collective-permute-start | bytes 774152 | tf_op jit(solution)/shard_map/ppermute | solution.py:651
  89.3 9.2 %collective-permute-start.21 = (bf16[84,1536]{1,0:T(8,128)(2,1)S(1)}, bf16[84,1536]{1,0:T(8,128)(2,1)S(1)}, u32[]{:S(2)}, u32[]{:S(2)}) collective-permute-start(bf16[84,1536]{1,0:T(8,128)(2,1)S(1)} %reduce_second.2), channel_id=1, source_target_pairs={{0,8},{24,16},{1,9},{25,17},{2,10},{26,18},{3,11},{27,19},{4,12},{... | collective-permute-start | bytes 774152 | tf_op jit(solution)/shard_map/ppermute | solution.py:652
  91.5 7.0 %collective-permute-start.22 = (bf16[84,1536]{1,0:T(8,128)(2,1)S(1)}, bf16[84,1536]{1,0:T(8,128)(2,1)S(1)}, u32[]{:S(2)}, u32[]{:S(2)}) collective-permute-start(bf16[84,1536]{1,0:T(8,128)(2,1)S(1)} %reduce_second.2), channel_id=1, source_target_pairs={{8,16},{16,8},{9,17},{17,9},{10,18},{18,10},{11,19},{19,11},{12,20... | collective-permute-start | bytes 774152 | tf_op jit(solution)/shard_map/ppermute | solution.py:651
  93.6 10.7 %copy-start.4 = (f32[84,128]{1,0:T(8,128)S(1)}, f32[84,128]{1,0:T(8,128)}, u32[]{:S(2)}) copy-start(f32[84,128]{1,0:T(8,128)} %constant.24.clone.cosine) | copy-start | bytes 129028
  93.6 10.7 %copy-start.5 = (f32[84,128]{1,0:T(8,128)S(1)}, f32[84,128]{1,0:T(8,128)}, u32[]{:S(2)}) copy-start(f32[84,128]{1,0:T(8,128)} %constant.25.clone.sine) | copy-start | bytes 129028
  93.6 10.7 %copy-start.8 = (s32[6]{0:T(128)S(1)}, s32[6]{0:T(128)}, u32[]{:S(2)}) copy-start(s32[6]{0:T(128)} %counts.1) | copy-start | bytes 76
  93.7 10.6 %collective-permute-start.28 = (bf16[84,1536]{1,0:T(8,128)(2,1)S(1)}, bf16[84,1536]{1,0:T(8,128)(2,1)S(1)}, u32[]{:S(2)}, u32[]{:S(2)}) collective-permute-start(bf16[84,1536]{1,0:T(8,128)(2,1)S(1)} %get-tuple-element.138), channel_id=1, source_target_pairs={{0,8},{8,0},{16,24},{24,16},{1,9},{9,1},{17,25},{25,17},{2,10},{10... | collective-permute-start | bytes 774152 | tf_op jit(solution)/shard_map/ppermute | solution.py:661
  96.5 7.8 %collective-permute-start.29 = (bf16[84,1536]{1,0:T(8,128)(2,1)S(1)}, bf16[84,1536]{1,0:T(8,128)(2,1)S(1)}, u32[]{:S(2)}, u32[]{:S(2)}) collective-permute-start(bf16[84,1536]{1,0:T(8,128)(2,1)S(1)} %get-tuple-element.139), channel_id=1, source_target_pairs={{8,16},{16,8},{9,17},{17,9},{10,18},{18,10},{11,19},{19,11},{12,20... | collective-permute-start | bytes 774152 | tf_op jit(solution)/shard_map/ppermute | solution.py:660
  98.6 11.2 %collective-permute-start.23 = (bf16[84,1536]{1,0:T(8,128)(2,1)S(1)}, bf16[84,1536]{1,0:T(8,128)(2,1)S(1)}, u32[]{:S(2)}, u32[]{:S(2)}) collective-permute-start(bf16[84,1536]{1,0:T(8,128)(2,1)S(1)} %get-tuple-element.133), channel_id=1, source_target_pairs={{0,8},{8,0},{16,24},{24,16},{1,9},{9,1},{17,25},{25,17},{2,10},{10... | collective-permute-start | bytes 774152 | tf_op jit(solution)/shard_map/ppermute | solution.py:661
  102.3 7.5 %collective-permute-start.24 = (bf16[84,1536]{1,0:T(8,128)(2,1)S(1)}, bf16[84,1536]{1,0:T(8,128)(2,1)S(1)}, u32[]{:S(2)}, u32[]{:S(2)}) collective-permute-start(bf16[84,1536]{1,0:T(8,128)(2,1)S(1)} %get-tuple-element.134), channel_id=1, source_target_pairs={{8,16},{16,8},{9,17},{17,9},{10,18},{18,10},{11,19},{19,11},{12,20... | collective-permute-start | bytes 774152 | tf_op jit(solution)/shard_map/ppermute | solution.py:660
